TPU v7x, 256 devices: a whole 4x4x8 slice. The times are simulated.
256 devices in a mesh: inst: 32 (over x, y, core), head: 8 (over z).
Axes of the slice: x: 4, y: 4, z: 8, core: 2. Of those that a mesh axis runs over, the one named last changes fastest.
Arguments:
- query: bfloat16 [2, 8, 64, 128], P(None, None, 'head')
- new_keys: bfloat16 [2, 8, 8, 128], P(None, None, 'head'), as said below
- new_values: bfloat16 [2, 8, 8, 128], P(None, None, 'head'), may hold values from -24 to 24
- cache_keys: bfloat16 [2048, 128, 8, 128], P('inst', None, 'head'), as said below
- cache_values: bfloat16 [2048, 128, 8, 128], P('inst', None, 'head'), may hold values from -24 to 24
- signs: int32 [8, 128], P('head'), may hold values from 0 to 1
- block_req: int32 [2048], replicated, may hold values from 0 to 7, as said below
- block_fill: int32 [2048], replicated, may hold values from 1 to 128, as said below
- dest_inst: int32 [2048], replicated, may hold values from 0 to 31, as said below
- new_slot: int32 [2048], replicated, may hold values from 0 to 63, as said below
- out_weight: bfloat16 [8192, 8192], P('head', 'inst'), may hold values from -0.125 to 0.125
Outputs:
- layer_out: bfloat16 [2, 8, 8192], P(None, None, 'inst')
- moved_keys: bfloat16 [2048, 128, 8, 128], P('inst', None, 'head')
- moved_values: bfloat16 [2048, 128, 8, 128], P('inst', None, 'head')
Inputs may be any that keep to these rules, and one draw needn't show every extreme that they name: `new_keys`: keys of the new tokens. `cache_keys`: rotated cached keys; positions at or after a block's fill hold stale entries. `block_req`: every request holds two blocks or more. `block_fill`: one block of each request may be partly live; all its other blocks hold 128 live positions. `dest_inst`: half of the instances are released: each of them sends exactly 4 of its blocks to every kept instance and keeps none; every kept instance keeps all its own blocks; the first and the last instance are always kept. `new_slot`: for a moved block its row among the 64 rows of its new instance, every row of a kept instance taken by exactly one moved block; for a block that stays, its own slot on its instance.
All inputs are finite; a program needn't handle non-finite values.
Results may differ from a plain program's by a relative error of at most 0.02.
Values may be sent and summed in bfloat16 or wider, within the bound.
A program may use at most 64 MiB of HBM per device.

v0:
```python
import math

import jax
import jax.numpy as jnp
from jax import lax
from jax.sharding import PartitionSpec as P

NEG_FILL = -1e30
HIGHEST = lax.Precision.HIGHEST


def combined_all(shard, axis, combine):
    everything = jax.tree.map(lambda part: lax.all_gather(part, axis), shard)
    initial = jax.tree.map(lambda part: part[0], everything)

    def hop(k, so_far):
        return combine(so_far, jax.tree.map(lambda part: part[k], everything))

    return lax.fori_loop(1, lax.axis_size(axis), hop, initial)


def hadamard_matrix(order_size):
    index_row = jnp.arange(order_size, dtype=jnp.int32)
    common = jnp.bitwise_and(index_row[:, None], index_row[None, :])
    parity = jnp.zeros((order_size, order_size), jnp.int32)
    for bit_index in range(order_size.bit_length() - 1):
        parity = parity + jnp.bitwise_and(jnp.right_shift(common, bit_index), 1)
    return (1 - 2 * jnp.bitwise_and(parity, 1)).astype(jnp.float32)


def rotation_tables(signs, order_size):
    sign_values = (2 * signs - 1).astype(jnp.float32)
    return sign_values[:, :, None] * hadamard_matrix(order_size)[None, :, :] / math.sqrt(order_size)


def block_partials(q_low, key_blocks, value_blocks, req_rows, fill_rows, alive_rows, score_scale):
    req_count = q_low.shape[1]
    block_tokens = key_blocks.shape[1]
    query_rows = jnp.take(q_low, req_rows, axis=1)
    scores = (
        jnp.einsum("sbkgd,btkd->sbkgt", query_rows, key_blocks, preferred_element_type=jnp.float32)
        * score_scale
    )
    positions = jnp.arange(block_tokens, dtype=jnp.int32)
    token_live = (positions[None, :] < fill_rows[:, None]) & alive_rows[:, None]
    live_full = token_live[None, :, None, None, :]
    masked = jnp.where(live_full, scores, NEG_FILL)
    block_max = jnp.max(masked, axis=-1)
    exp_terms = jnp.where(live_full, jnp.exp(masked - block_max[..., None]), 0.0)
    block_total = jnp.sum(exp_terms, axis=-1)
    block_sum = jnp.einsum(
        "sbkgt,btkd->sbkgd",
        exp_terms.astype(jnp.bfloat16),
        value_blocks,
        preferred_element_type=jnp.float32,
    )
    requests = jnp.arange(req_count, dtype=jnp.int32)
    owner = (req_rows[:, None] == requests[None, :]) & alive_rows[:, None]
    owner_max = jnp.where(owner[None, :, None, None, :], block_max[..., None], NEG_FILL)
    req_max = jnp.moveaxis(jnp.max(owner_max, axis=1), -1, 1)
    block_ref = jnp.take(req_max, req_rows, axis=1)
    factor = jnp.exp(block_max - block_ref)
    owner_f = owner.astype(jnp.float32)
    local_total = jnp.einsum("sbkg,br->srkg", block_total * factor, owner_f, precision=HIGHEST)
    local_sum = jnp.einsum(
        "sbkgd,br->srkgd", block_sum * factor[..., None], owner_f, precision=HIGHEST
    )
    return (req_max, local_total, local_sum)


def combine_partials(earlier_part, later_part):
    max_early, total_early, sum_early = earlier_part
    max_late, total_late, sum_late = later_part
    joined_max = jnp.maximum(max_early, max_late)
    factor_early = jnp.exp(max_early - joined_max)
    factor_late = jnp.exp(max_late - joined_max)
    joined_total = total_early * factor_early + total_late * factor_late
    joined_sum = sum_early * factor_early[..., None] + sum_late * factor_late[..., None]
    return (joined_max, joined_total, joined_sum)


def shards(
    query,
    new_keys,
    new_values,
    cache_keys,
    cache_values,
    signs,
    block_req,
    block_fill,
    dest_inst,
    new_slot,
    out_weight,
):
    inst_count = lax.axis_size("inst")
    own_index = lax.axis_index("inst")
    slot_count, block_tokens, kv_heads, head_dim = cache_keys.shape
    step_count, req_count, query_heads, _ = query.shape
    group_size = query_heads // kv_heads
    keep_count = inst_count // 2
    pair_count = slot_count // keep_count
    score_scale = 1.0 / math.sqrt(head_dim)
    zero_low = jnp.zeros((), jnp.bfloat16)
    rotation = rotation_tables(signs, head_dim)
    query_f = query.astype(jnp.float32).reshape(
        step_count, req_count, kv_heads, group_size, head_dim
    )
    q_rot = jnp.einsum("srkgi,kij->srkgj", query_f, rotation, precision=HIGHEST)
    q_low = q_rot.astype(jnp.bfloat16)
    peer_ids = jnp.arange(inst_count, dtype=jnp.int32)
    slot_ids = jnp.arange(slot_count, dtype=jnp.int32)
    rank_ids = jnp.arange(pair_count, dtype=jnp.int32)
    plan_dest = dest_inst.reshape(inst_count, slot_count)
    plan_slot = new_slot.reshape(inst_count, slot_count)
    plan_req = block_req.reshape(inst_count, slot_count)
    plan_fill = block_fill.reshape(inst_count, slot_count)
    to_peer = (plan_dest[:, :, None] == peer_ids[None, None, :]).astype(jnp.int32)
    plan_rank = jnp.sum(jnp.cumsum(to_peer, axis=1) * to_peer, axis=2) - 1
    plan_moved = plan_dest != peer_ids[:, None]
    own_dest = lax.dynamic_index_in_dim(plan_dest, own_index, 0, keepdims=False)
    own_rank = lax.dynamic_index_in_dim(plan_rank, own_index, 0, keepdims=False)
    own_moved = lax.dynamic_index_in_dim(plan_moved, own_index, 0, keepdims=False)
    own_req = lax.dynamic_index_in_dim(plan_req, own_index, 0, keepdims=False)
    own_fill = lax.dynamic_index_in_dim(plan_fill, own_index, 0, keepdims=False)
    send_match = (
        own_moved[None, None, :]
        & (own_dest[None, None, :] == peer_ids[:, None, None])
        & (own_rank[None, None, :] == rank_ids[None, :, None])
    )
    send_valid = jnp.any(send_match, axis=2).reshape(-1)
    send_index = jnp.sum(jnp.where(send_match, slot_ids[None, None, :], 0), axis=2).reshape(-1)
    send_keys = jnp.where(
        send_valid[:, None, None, None], jnp.take(cache_keys, send_index, axis=0), zero_low
    )
    send_values = jnp.where(
        send_valid[:, None, None, None], jnp.take(cache_values, send_index, axis=0), zero_low
    )
    got_keys, got_values = (
        lax.all_to_all(send_keys, "inst", split_axis=0, concat_axis=0, tiled=True),
        lax.all_to_all(send_values, "inst", split_axis=0, concat_axis=0, tiled=True),
    )
    recv_match = (
        plan_moved[:, None, :]
        & (plan_dest[:, None, :] == own_index)
        & (plan_rank[:, None, :] == rank_ids[None, :, None])
    )
    recv_valid = jnp.any(recv_match, axis=2).reshape(-1)
    recv_slot = jnp.sum(jnp.where(recv_match, plan_slot[:, None, :], 0), axis=2).reshape(-1)
    global_ids = peer_ids[:, None, None] * slot_count + slot_ids[None, None, :]
    recv_block = jnp.sum(jnp.where(recv_match, global_ids, 0), axis=2).reshape(-1)
    row_ids = jnp.arange(inst_count * pair_count, dtype=jnp.int32)
    place_match = recv_valid[None, :] & (recv_slot[None, :] == slot_ids[:, None])
    place_has = jnp.any(place_match, axis=1)
    place_row = jnp.sum(jnp.where(place_match, row_ids[None, :], 0), axis=1)
    moved_block = jnp.sum(jnp.where(place_match, recv_block[None, :], 0), axis=1)
    moved_keys = jnp.where(
        place_has[:, None, None, None], jnp.take(got_keys, place_row, axis=0), zero_low
    )
    moved_values = jnp.where(
        place_has[:, None, None, None], jnp.take(got_values, place_row, axis=0), zero_low
    )
    kept_part = block_partials(
        q_low, cache_keys, cache_values, own_req, own_fill, jnp.logical_not(own_moved), score_scale
    )
    moved_req_rows = jnp.take(block_req, moved_block, axis=0)
    moved_fill_rows = jnp.take(block_fill, moved_block, axis=0)
    arrived_part = block_partials(
        q_low, moved_keys, moved_values, moved_req_rows, moved_fill_rows, place_has, score_scale
    )
    partial_rows = combine_partials(kept_part, arrived_part)
    cache_max, cache_total, cache_sum = combined_all(partial_rows, "inst", combine_partials)
    new_rot = jnp.einsum(
        "srki,kij->srkj", new_keys.astype(jnp.float32), rotation, precision=HIGHEST
    )
    value_rot = jnp.einsum(
        "srki,kij->srkj", new_values.astype(jnp.float32), rotation, precision=HIGHEST
    )
    new_scores = jnp.einsum("srkgd,jrkd->srkgj", q_rot, new_rot, precision=HIGHEST) * score_scale
    step_ids = jnp.arange(step_count, dtype=jnp.int32)
    causal = (step_ids[None, :] <= step_ids[:, None])[:, None, None, None, :]
    new_scores = jnp.where(causal, new_scores, NEG_FILL)
    joined_max = jnp.maximum(cache_max, jnp.max(new_scores, axis=-1))
    cache_factor = jnp.exp(cache_max - joined_max)
    new_weights = jnp.where(causal, jnp.exp(new_scores - joined_max[..., None]), 0.0)
    denominator = cache_factor * cache_total + jnp.sum(new_weights, axis=-1)
    numerator = cache_factor[..., None] * cache_sum + jnp.einsum(
        "srkgj,jrkd->srkgd", new_weights, value_rot, precision=HIGHEST
    )
    attended_rot = numerator / denominator[..., None]
    attended = jnp.einsum("srkgj,kij->srkgi", attended_rot, rotation, precision=HIGHEST).astype(
        jnp.bfloat16
    )
    flat_rows = attended.reshape(step_count * req_count, query_heads * head_dim)
    head_terms = jnp.dot(flat_rows, out_weight, preferred_element_type=jnp.float32)
    projected = lax.psum(head_terms, "head")
    layer_out = projected.astype(jnp.bfloat16).reshape(step_count, req_count, out_weight.shape[1])
    return (layer_out, moved_keys, moved_values)


def solution(mesh):
    placed = (
        P(None, None, "head", None),
        P(None, None, "head", None),
        P(None, None, "head", None),
        P("inst", None, "head", None),
        P("inst", None, "head", None),
        P("head", None),
        P(),
        P(),
        P(),
        P(),
        P("head", "inst"),
    )
    return jax.shard_map(
        shards,
        mesh=mesh,
        in_specs=placed,
        out_specs=(
            P(None, None, "inst"),
            P("inst", None, "head", None),
            P("inst", None, "head", None),
        ),
        check_vma=False,
    )
```

profile of v0, /device:TPU:8, one launch (start us, length us, event | category | flops | bytes accessed | tf_op | source)
XLA Modules:
  0.0 287.9 jit_solution(12599168033170191926)
XLA Ops:
  7.2 0.9 reshape.727
  8.2 0.8 reshape.728
  9.0 1.7 select_reduce_fusion
  11.5 3.1 %gather_fusion.3 = bf16[128,128,128]{2,1,0:T(8,128)(2,1)} fusion(bf16[64,128,128]{2,1,0:T(8,128)(2,1)S(1)} %bitcast.475, s32[1024]{0:T(1024)S(1)} %pad_clamp_fusion.2), kind=kCustom, calls=%fused_computation.2.clone | custom fusion | bytes 8389120 | tf_op jit(solution)/shard_map/jit(_take)/gather | solution.py:133
  14.6 4.6 %gather_fusion.8 = bf16[128,128,128]{2,1,0:T(8,128)(2,1)} fusion(bf16[64,128,128]{2,1,0:T(8,128)(2,1)} %bitcast.476, s32[1024]{0:T(1024)S(1)} %pad_clamp_fusion.2), kind=kCustom, calls=%fused_computation.7.clone | custom fusion | bytes 8389120 | tf_op jit(solution)/shard_map/jit(_take)/gather | solution.py:136
  19.4 6.3 %fusion.5 = (bf16[128,128,1,128]{3,1,2,0:T(8,128)(2,1)}, bf16[128,128,1,128]{3,1,2,0:T(8,128)(2,1)}) fusion(bf16[128,128,128]{2,1,0:T(8,128)(2,1)} %gather_fusion.8, pred[128]{0:T(512)(128)(4,1)S(1)} %compare_and_fusion.3, pred[128]{0:T(512)(128)(4,1)S(1)} %broadcast_in_dim.279, bf16[128,128,128]{2,1,0:T(8,128)(2,1)} %gather_fusion.3), kind=kLoop, calls=%fused_computation.21 | loop fusion | flops 8388608 | bytes 16777472 | tf_op jit(solution)/shard_map/jit(_where)/select_n | solution.py:135
  25.7 7.7 %all-to-all-start.1 = ((bf16[128,128,1,128]{3,1,2,0:T(8,128)(2,1)}), bf16[128,128,1,128]{3,1,2,0:T(8,128)(2,1)}, u32[]{:S(2)}, u32[]{:S(2)}) async-start(bf16[128,128,1,128]{3,1,2,0:T(8,128)(2,1)} %get-tuple-element.274), calls=%async_computation.1 | async-start | bytes 8388608 | tf_op jit(solution)/shard_map/all_to_all | solution.py:140
  34.9 0.8 gather_fusion.1
  35.6 52.4 %all-to-all-done.1 = bf16[128,128,1,128]{3,1,2,0:T(8,128)(2,1)} async-done(((bf16[128,128,1,128]{3,1,2,0:T(8,128)(2,1)}), bf16[128,128,1,128]{3,1,2,0:T(8,128)(2,1)}, u32[]{:S(2)}, u32[]{:S(2)}) %all-to-all-start.1) | async-done | bytes 4194336 | tf_op jit(solution)/shard_map/all_to_all | solution.py:140
  88.0 5.0 %all-to-all-start = ((bf16[128,128,1,128]{3,1,2,0:T(8,128)(2,1)}), bf16[128,128,1,128]{3,1,2,0:T(8,128)(2,1)}, u32[]{:S(2)}, u32[]{:S(2)}) async-start(bf16[128,128,1,128]{3,1,2,0:T(8,128)(2,1)} %get-tuple-element.275), calls=%async_computation | async-start | bytes 8388608 | tf_op jit(solution)/shard_map/all_to_all | solution.py:139
  93.3 0.8 gather_fusion.2
  94.5 0.6 copy-done.4
  95.1 1.4 gather_fusion.5
  96.5 0.7 gather_fusion
  97.3 1.4 fusion.238
  98.9 0.7 gather_fusion.6
  100.4 2.3 fusion.44
  102.7 4.3 %gather_fusion.9 = bf16[64,128,128]{2,1,0:T(8,128)(2,1)} fusion(bf16[128,128,128]{2,1,0:T(8,128)(2,1)} %bitcast.84, s32[1024]{0:T(1024)S(1)} %pad_clamp_fusion.1), kind=kCustom, calls=%fused_computation.8.clone | custom fusion | bytes 4194560 | tf_op jit(solution)/shard_map/jit(_take)/gather | solution.py:160
  107.1 40.5 %all-to-all-done = bf16[128,128,1,128]{3,1,2,0:T(8,128)(2,1)} async-done(((bf16[128,128,1,128]{3,1,2,0:T(8,128)(2,1)}), bf16[128,128,1,128]{3,1,2,0:T(8,128)(2,1)}, u32[]{:S(2)}, u32[]{:S(2)}) %all-to-all-start) | async-done | bytes 4194336 | tf_op jit(solution)/shard_map/all_to_all | solution.py:139
  147.5 4.3 %gather_fusion.4 = bf16[64,128,128]{2,1,0:T(8,128)(2,1)} fusion(bf16[128,128,128]{2,1,0:T(8,128)(2,1)} %bitcast.31, s32[1024]{0:T(1024)S(1)} %pad_clamp_fusion.1), kind=kCustom, calls=%fused_computation.3.clone | custom fusion | bytes 4194560 | tf_op jit(solution)/shard_map/jit(_take)/gather | solution.py:157
  151.9 3.0 %fusion.237 = (f32[2,64,8]{2,0,1:T(2,128)S(1)}, f32[2,64,1,8,128]{4,3,0,1,2:T(8,128)S(1)}) fusion(bf16[64,2,8,128]{3,2,1,0:T(8,128)(2,1)} %gather_fusion.5, pred[64]{0:T(512)(128)(4,1)S(1)} %get-tuple-element.257, bf16[64,128,128]{2,1,0:T(8,128)(2,1)} %gather_fusion.4, pred[64]{0:T(512)(128)(4,1)S(1)} %compare_and_fusion.2, pred[64]{0:T(512)(128)(4,1)S(1)} %fusion.164, ...), kind=kOutput, calls=%fused_computation.294 | convolution fusion | flops 36174848 | bytes 2896064 | tf_op jit(solution)/shard_map/sbkgd,btkd->sbkgt/dot_general | solution.py:41
  154.9 0.4 fusion.83
  155.6 0.8 gather_fusion.7
  156.3 0.8 fusion.234
  157.2 2.2 fusion.38
  160.3 0.6 copy.185
  161.4 1.0 fusion.239
  163.0 21.8 %all-gather.1 = f32[64,8,1,8]{3,1,2,0:T(8,128)S(1)} all-gather(f32[2,8,1,8]{3,1,2,0:T(8,128)S(1)} %copy.178), channel_id=3, replica_groups=mesh['inst'=32,'head'=8] {'inst'}, dimensions={0}, use_global_device_ids=true | all-gather | bytes 16896 | tf_op jit(solution)/shard_map/all_gather | solution.py:13
  184.8 24.7 %all-gather = f32[64,8,1,8]{3,1,2,0:T(8,128)S(1)} all-gather(f32[2,8,1,8]{3,1,2,0:T(8,128)S(1)} %copy.169), channel_id=2, replica_groups=mesh['inst'=32,'head'=8] {'inst'}, dimensions={0}, use_global_device_ids=true | all-gather | bytes 16896 | tf_op jit(solution)/shard_map/all_gather | solution.py:13
  209.6 4.0 %fusion.73 = (bf16[64,128,1,128]{3,1,2,0:T(8,128)(2,1)}, bf16[64,128,1,128]{3,1,2,0:T(8,128)(2,1)}) fusion(bf16[64,128,128]{2,1,0:T(8,128)(2,1)} %gather_fusion.9, pred[64]{0:T(512)(128)(4,1)S(1)} %copy-done.19, pred[64]{0:T(512)(128)(4,1)S(1)} %copy-done.12, bf16[64,128,128]{2,1,0:T(8,128)(2,1)} %gather_fusion.4), kind=kLoop, calls=%fused_computation.72 | loop fusion | flops 4194304 | bytes 8388736
  213.6 0.9 slice.37
  214.5 32.2 %while.19 = (s32[]{:T(128)}, f32[2,8,1,8]{3,1,0,2:T(8,128)S(1)}, f32[2,8,1,8]{3,1,0,2:T(8,128)S(1)}, f32[2,8,1,8,128]{4,3,2,1,0:T(8,128)S(1)}, f32[32,2,8,1,8]{4...) while((s32[]{:T(128)}, f32[2,8,1,8]{3,1,0,2:T(8,128)S(1)}, ...), condition=%wide.region_17.23_spmd, body=%wide.region_16.22_spmd.sunk | while | flops 50053 | bytes 204443 | solution.py:19
  214.5 1.0 fusion.248
  215.5 1.0 fusion.248
  216.6 1.0 fusion.248
  217.6 1.0 fusion.248
  218.7 1.0 fusion.248
  219.7 1.0 fusion.248
  220.7 1.0 fusion.248
  221.8 1.0 fusion.248
  222.8 1.0 fusion.248
  223.9 1.0 fusion.248
  224.9 1.0 fusion.248
  225.9 1.0 fusion.248
  227.0 1.0 fusion.248
  228.0 1.0 fusion.248
  229.1 1.0 fusion.248
  230.1 1.0 fusion.248
  231.1 1.0 fusion.248
  232.2 1.0 fusion.248
  233.2 1.0 fusion.248
  234.3 1.0 fusion.248
  235.3 1.0 fusion.248
  236.3 1.0 fusion.248
  237.4 1.0 fusion.248
  238.4 1.0 fusion.248
  239.5 1.0 fusion.248
  240.5 1.0 fusion.248
  241.5 1.0 fusion.248
  242.6 1.0 fusion.248
  243.6 1.0 fusion.248
  244.7 1.0 fusion.248
  245.7 1.0 fusion.248
  247.8 33.3 %psum.7 = bf16[16,256]{1,0:T(8,128)(2,1)} all-reduce(f32[16,256]{1,0:T(8,128)S(1)} %fusion.150), channel_id=1, replica_groups=mesh['inst'=32,'head'=8] {'head'}, use_global_device_ids=true, to_apply=%region_20.26 | all-reduce | flops 4096 | bytes 24576 | tf_op jit(solution)/shard_map/psum | solution.py:195
  (227 shorter events, 8.5 us)
Async XLA Ops:
  7.2 4.3 %copy-start = (bf16[64,128,1,128]{3,1,2,0:T(8,128)(2,1)S(1)}, bf16[64,128,1,128]{3,1,2,0:T(8,128)(2,1)}, u32[]{:S(2)}) copy-start(bf16[64,128,1,128]{3,1,2,0:T(8,128)(2,1)} %param.26) | copy-start | bytes 6291460
  9.0 89.7 %copy-start.6 = (pred[64]{0:T(512)(128)(4,1)}, pred[64]{0:T(512)(128)(4,1)S(1)}, u32[]{:S(2)}) copy-start(pred[64]{0:T(512)(128)(4,1)S(1)} %get-tuple-element.253) | copy-start | bytes 196
  25.7 7.8 %copy-start.15 = (s32[2048]{0:T(1024)S(1)}, s32[2048]{0:T(1024)}, u32[]{:S(2)}) copy-start(s32[2048]{0:T(1024)} %param.32) | copy-start | bytes 24580
  25.7 9.1 %copy-start.2 = (s32[2048]{0:T(1024)S(1)}, s32[2048]{0:T(1024)}, u32[]{:S(2)}) copy-start(s32[2048]{0:T(1024)} %param.29) | copy-start | bytes 24580
  25.7 62.3 %all-to-all-start.1 = ((bf16[128,128,1,128]{3,1,2,0:T(8,128)(2,1)}), bf16[128,128,1,128]{3,1,2,0:T(8,128)(2,1)}, u32[]{:S(2)}, u32[]{:S(2)}) async-start(bf16[128,128,1,128]{3,1,2,0:T(8,128)(2,1)} %get-tuple-element.274), calls=%async_computation.1 | async-start | bytes 8388608 | tf_op jit(solution)/shard_map/all_to_all | solution.py:140
  88.0 5.2 %copy-start.1 = (s32[2048]{0:T(1024)S(1)}, s32[2048]{0:T(1024)}, u32[]{:S(2)}) copy-start(s32[2048]{0:T(1024)} %param.30) | copy-start | bytes 24580
  88.0 6.2 %copy-start.23 = (s32[1,128]{1,0:T(1,128)S(1)}, s32[1,128]{1,0:T(1,128)}, u32[]{:S(2)}) copy-start(s32[1,128]{1,0:T(1,128)} %param.28) | copy-start | bytes 1540
  88.0 6.2 %copy-start.20 = (bf16[2,8,8,128]{3,2,1,0:T(8,128)(2,1)S(1)}, bf16[2,8,8,128]{3,2,1,0:T(8,128)(2,1)}, u32[]{:S(2)}) copy-start(bf16[2,8,8,128]{3,2,1,0:T(8,128)(2,1)} %param.23) | copy-start | bytes 98308
  88.0 59.5 %all-to-all-start = ((bf16[128,128,1,128]{3,1,2,0:T(8,128)(2,1)}), bf16[128,128,1,128]{3,1,2,0:T(8,128)(2,1)}, u32[]{:S(2)}, u32[]{:S(2)}) async-start(bf16[128,128,1,128]{3,1,2,0:T(8,128)(2,1)} %get-tuple-element.275), calls=%async_computation | async-start | bytes 8388608 | tf_op jit(solution)/shard_map/all_to_all | solution.py:139
  93.0 120.6 %all-gather.5.cloned.1.call-start = ((), (), s32[]{:S(2)}) async-start(), calls=%async_computation.2 | async-start | bytes 2162688 | tf_op jit(solution)/shard_map/all_gather | solution.py:13
  93.3 6.5 %copy-start.13 = (s32[64]{0:T(128)}, s32[64]{0:T(128)S(1)}, u32[]{:S(2)}) copy-start(s32[64]{0:T(128)S(1)} %get-tuple-element.258) | copy-start | bytes 772
  93.3 58.6 %copy-start.17 = (pred[64]{0:T(512)(128)(4,1)}, pred[64]{0:T(512)(128)(4,1)S(1)}, u32[]{:S(2)}) copy-start(pred[64]{0:T(512)(128)(4,1)S(1)} %get-tuple-element.257) | copy-start | bytes 196
  94.1 4.6 %copy-start.8 = (s32[64]{0:T(128)}, s32[64]{0:T(128)S(1)}, u32[]{:S(2)}) copy-start(s32[64]{0:T(128)S(1)} %get-tuple-element.256) | copy-start | bytes 772
  94.2 4.4 %copy-start.16 = (s32[1024]{0:T(1024)}, s32[1024]{0:T(1024)S(1)}, u32[]{:S(2)}) copy-start(s32[1024]{0:T(1024)S(1)} %pad_clamp_fusion) | copy-start | bytes 12292
  94.2 2.3 copy-start.24
  94.5 0.6 copy-start.4
  99.7 52.2 %copy-start.10 = (pred[64]{0:T(512)(128)(4,1)}, pred[64]{0:T(512)(128)(4,1)S(1)}, u32[]{:S(2)}) copy-start(pred[64]{0:T(512)(128)(4,1)S(1)} %fusion.164) | copy-start | bytes 196
  99.7 52.1 %copy-start.18 = (pred[64]{0:T(512)(128)(4,1)}, pred[64]{0:T(512)(128)(4,1)S(1)}, u32[]{:S(2)}) copy-start(pred[64]{0:T(512)(128)(4,1)S(1)} %compare_and_fusion.2) | copy-start | bytes 196
  157.1 2.3 copy-start.7
  157.1 2.3 copy-start.9
  157.1 2.8 copy-start.11
  157.1 2.8 copy-start.14
  157.1 3.9 %copy-start.21 = (bf16[2,8,1,128]{3,1,2,0:T(8,128)(2,1)S(1)}, bf16[2,8,1,128]{3,1,2,0:T(8,128)(2,1)}, u32[]{:S(2)}) copy-start(bf16[2,8,1,128]{3,1,2,0:T(8,128)(2,1)} %param.24) | copy-start | bytes 12292
  157.2 3.9 %copy-start.25 = (f32[128]{0:T(128)S(1)}, f32[128]{0:T(128)}, u32[]{:S(2)}) copy-start(f32[128]{0:T(128)} %copy-done.24) | copy-start | bytes 1540
  157.2 4.0 %copy-start.22 = (bf16[2,8,1,128]{3,1,2,0:T(8,128)(2,1)S(1)}, bf16[2,8,1,128]{3,1,2,0:T(8,128)(2,1)}, u32[]{:S(2)}) copy-start(bf16[2,8,1,128]{3,1,2,0:T(8,128)(2,1)} %param.25) | copy-start | bytes 12292
  159.4 2.0 copy-start.5
  159.4 50.1 %copy-start.12 = (pred[64]{0:T(512)(128)(4,1)S(1)}, pred[64]{0:T(512)(128)(4,1)}, u32[]{:S(2)}) copy-start(pred[64]{0:T(512)(128)(4,1)} %copy-done.10) | copy-start | bytes 196
  159.4 50.1 %copy-start.19 = (pred[64]{0:T(512)(128)(4,1)S(1)}, pred[64]{0:T(512)(128)(4,1)}, u32[]{:S(2)}) copy-start(pred[64]{0:T(512)(128)(4,1)} %copy-done.18) | copy-start | bytes 196
  213.5 33.7 %copy-start.26 = (f32[128]{0:T(128)S(1)}, f32[128]{0:T(128)}, u32[]{:S(2)}) copy-start(f32[128]{0:T(128)} %copy-done.24) | copy-start | bytes 1540
  213.5 34.0 %copy-start.3 = (bf16[1024,256]{1,0:T(8,128)(2,1)S(1)}, bf16[1024,256]{1,0:T(8,128)(2,1)}, u32[]{:S(2)}) copy-start(bf16[1024,256]{1,0:T(8,128)(2,1)} %param.33) | copy-start | bytes 1572868
Sparse Core Ops, SparseCore 0:
  161.1 48.7 all-gather.4
where the time goes:
time: 290 us; the launch traced here: 288 us
  waiting for transfers between devices  92.9 us (32%)
  blocking collectives  79.8 us (28%)
  other arithmetic  46.1 us (16%)
  local copies, waits for them, and re-layouts  27.3 us (9%)
  between operations  14.7 us (5%)
  starting transfers between devices  12.9 us (4%)
  matrix products  12.7 us (4%)
    all_to_all x1, waiting for transfers between devices, shards(): lax.all_to_all(send_values, 'inst', split_axis=0, concat_axis=0, tiled=True)  52.4 us
    all_gather x2, blocking collectives, combined_all(): everything = jax.tree.map(lambda part: lax.all_gather(part, axis), shard)  46.5 us
    all_to_all x1, waiting for transfers between devices, shards(): lax.all_to_all(send_keys, 'inst', split_axis=0, concat_axis=0, tiled=True)  40.5 us
    psum x1, blocking collectives, shards(): projected = lax.psum(head_terms, 'head')  33.3 us
    add x31, other arithmetic, combine_partials(): sum_early * factor_early[..., None] + sum_late * factor_late[..., None]  29.6 us
    all_to_all x1, starting transfers between devices, shards(): lax.all_to_all(send_values, 'inst', split_axis=0, concat_axis=0, tiled=True)  7.73 us
    select_n x1, other arithmetic, shards(): jnp.where(send_valid[:, None, None, None], jnp.take(cache_values, send_in...  6.35 us
  transfers between devices with their start and end apart: 3, of which 2 were waited for; matrix products, arithmetic and copies ran while one was open for 7% of the time, Pallas kernels for 0%

commit v1 on v0

v1 whole, which is shorter than its diff:
```python
import functools
import math

import jax
import jax.numpy as jnp
from jax import lax
from jax.experimental import pallas as pl
from jax.experimental.pallas import tpu as pltpu
from jax.sharding import PartitionSpec as P

NEG_FILL = -1e30
HIGHEST = lax.Precision.HIGHEST
MESH = pl.DeviceIdType.MESH
INST = 32
HEADS = 8
PER = 4
SLOTS = 64
BT = 128
HD = 128
ROWS = 128
CHUNK = 4


def hadamard(order_size):
    common = jnp.bitwise_and(
        lax.broadcasted_iota(jnp.int32, (order_size, order_size), 0),
        lax.broadcasted_iota(jnp.int32, (order_size, order_size), 1),
    )
    parity = common
    for shift in (4, 2, 1):
        parity = jnp.bitwise_xor(parity, jnp.right_shift(parity, shift))
    return (1 - 2 * jnp.bitwise_and(parity, 1)).astype(jnp.float32)


def remote(src, dst, send_sem, recv_sem, inst, head):
    return pltpu.make_async_remote_copy(
        src_ref=src,
        dst_ref=dst,
        send_sem=send_sem,
        recv_sem=recv_sem,
        device_id=(inst, head),
        device_id_type=MESH,
    )


def attend(plan_ref, q_low, kc, vc, scores, scale):
    row_req = lax.broadcasted_iota(jnp.int32, (ROWS, BT), 0) // 8 % 8
    token = lax.broadcasted_iota(jnp.int32, (ROWS, BT), 1)
    chunks = SLOTS // CHUNK

    def score_chunk(i, top):
        keys = kc[pl.ds(i * CHUNK, CHUNK)].reshape(CHUNK * BT, HD)
        s = lax.dot_general(
            q_low, keys, (((1,), (1,)), ((), ())), preferred_element_type=jnp.float32
        )
        for c in range(CHUNK):
            req = plan_ref[128 + i * CHUNK + c]
            fill = plan_ref[192 + i * CHUNK + c]
            live = (row_req == req) & (token < fill)
            part = jnp.where(live, s[:, c * BT : (c + 1) * BT] * scale, NEG_FILL)
            scores[i, :, c * BT : (c + 1) * BT] = part
            top = jnp.maximum(top, part)
        return top

    top = lax.fori_loop(0, chunks, score_chunk, jnp.full((ROWS, BT), NEG_FILL, jnp.float32))
    row_max = jnp.max(top, axis=1, keepdims=True)

    def value_chunk(i, carry):
        total, acc = carry
        p = jnp.exp(scores[i] - row_max)
        for c in range(CHUNK):
            total = total + p[:, c * BT : (c + 1) * BT]
        values = vc[pl.ds(i * CHUNK, CHUNK)].reshape(CHUNK * BT, HD)
        acc = acc + jnp.dot(p.astype(jnp.bfloat16), values, preferred_element_type=jnp.float32)
        return total, acc

    zero = jnp.zeros((ROWS, BT), jnp.float32)
    total, acc = lax.fori_loop(0, chunks, value_chunk, (zero, zero))
    return row_max, jnp.sum(total, axis=1, keepdims=True), acc


def finish_rows(parts, group, q_group, nk, nv, sign_row, rotate, scale):
    req, step = group % 8, group // 8
    part_max = parts[:, :, HD : HD + 1]
    part_total = parts[:, :, HD + 64 : HD + 65]
    cache_max = jnp.max(part_max, axis=0)
    factor = jnp.exp(part_max - cache_max[None])
    cache_total = jnp.sum(part_total * factor, axis=0)
    cache_sum = jnp.sum(parts[:, :, :HD] * factor, axis=0)
    new_scores = (
        lax.dot_general(q_group, nk, (((1,), (1,)), ((), ())), preferred_element_type=jnp.float32)
        * scale
    )
    col = lax.broadcasted_iota(jnp.int32, (8, 16), 1)
    causal = (col % 8 == req) & (col // 8 <= step)
    new_scores = jnp.where(causal, new_scores, NEG_FILL)
    joined_max = jnp.maximum(cache_max, jnp.max(new_scores, axis=1, keepdims=True))
    cache_factor = jnp.exp(cache_max - joined_max)
    weights = jnp.where(causal, jnp.exp(new_scores - joined_max), 0.0)
    denominator = cache_factor * cache_total + jnp.sum(weights, axis=1, keepdims=True)
    back = jnp.dot(
        cache_factor * cache_sum, rotate, precision=HIGHEST, preferred_element_type=jnp.float32
    )
    back = back * sign_row * (1.0 / math.sqrt(HD))
    fresh = jnp.dot(weights, nv, precision=HIGHEST, preferred_element_type=jnp.float32)
    return (back + fresh) / denominator


def layer_kernel(
    plan_ref,
    q_ref,
    nk_ref,
    nv_ref,
    signs_ref,
    w_ref,
    ck_ref,
    cv_ref,
    out_ref,
    rk_ref,
    rv_ref,
    kc,
    vc,
    sk,
    sv,
    scores,
    qf,
    part_send,
    part_recv,
    att,
    proj,
    load_sem,
    k_send,
    k_recv,
    v_send,
    v_recv,
    part_s,
    part_r,
    att_s,
    att_r,
    proj_s,
    proj_r,
):
    me = lax.axis_index("inst")
    head = lax.axis_index("head")
    chip, core = me // 2, me % 2
    scale = 1.0 / math.sqrt(HD)

    load_k = pltpu.make_async_copy(ck_ref, kc, load_sem.at[0])
    load_v = pltpu.make_async_copy(cv_ref, vc, load_sem.at[1])
    load_k.start()
    load_v.start()

    barrier = pltpu.get_barrier_semaphore()

    def greet_inst(o, _):
        pl.semaphore_signal(
            barrier, inc=1, device_id=(lax.rem(me + o, INST), head), device_id_type=MESH
        )
        return 0

    def greet_head(o, _):
        pl.semaphore_signal(
            barrier, inc=1, device_id=(me, lax.rem(head + o, HEADS)), device_id_type=MESH
        )
        return 0

    lax.fori_loop(1, INST, greet_inst, 0)
    lax.fori_loop(1, HEADS, greet_head, 0)

    sign_row = (2 * signs_ref[...] - 1).astype(jnp.float32)
    rotate = hadamard(HD)
    raw = q_ref[...].astype(jnp.float32)
    qf[...] = raw
    q_rot = jnp.dot(
        (raw * sign_row).astype(jnp.bfloat16),
        rotate.astype(jnp.bfloat16),
        preferred_element_type=jnp.float32,
    ) * (1.0 / math.sqrt(HD))
    q_low = q_rot.astype(jnp.bfloat16)

    load_k.wait()
    load_v.wait()
    pl.semaphore_wait(barrier, INST - 1 + HEADS - 1)

    def move(o):
        to = lax.rem(me + o, INST)
        return (
            remote(sk.at[o], rk_ref.at[me], k_send.at[o], k_recv.at[me], to, head),
            remote(sv.at[o], rv_ref.at[me], v_send.at[o], v_recv.at[me], to, head),
        )

    def arrived(o):
        src = lax.rem(me + o, INST)
        return (
            remote(sk.at[o], rk_ref.at[src], k_send.at[o], k_recv.at[src], src, head),
            remote(sv.at[o], rv_ref.at[src], v_send.at[o], v_recv.at[src], src, head),
        )

    def send_blocks(o, _):
        to = lax.rem(me + o, INST)
        for k in range(PER):
            b = plan_ref[to * PER + k]
            sk[o, k] = kc[b]
            sv[o, k] = vc[b]
        for copy in move(o):
            copy.start()
        return 0

    lax.fori_loop(1, INST, send_blocks, 0)

    row_max, row_total, acc = attend(plan_ref, q_low, kc, vc, scores, scale)
    lane = lax.broadcasted_iota(jnp.int32, (ROWS, HD), 1)
    part_send[:, :, :HD] = acc.reshape(16, 8, HD)
    part_send[:, :, HD:] = jnp.where(lane < 64, row_max, row_total).reshape(16, 8, HD)

    def part_copy(t):
        c = lax.rem(chip + t, 16)
        return remote(
            part_send.at[c], part_recv.at[me], part_s.at[t], part_r.at[me], 2 * c, head
        )

    def start_part(t, _):
        part_copy(t).start()
        return 0

    lax.fori_loop(1, 16, start_part, 0)

    @pl.when(core == 1)
    def _():
        part_copy(0).start()

    @pl.when(core == 0)
    def _():
        part_recv[me] = part_send[chip]

        def got_part(o, _):
            src = lax.rem(me + o, INST)
            remote(
                part_send.at[0], part_recv.at[src], part_s.at[0], part_r.at[src], src, head
            ).wait_recv()
            return 0

        lax.fori_loop(1, INST, got_part, 0)
        q_group = qf[pl.ds(pl.multiple_of(chip * 8, 8), 8)].astype(jnp.bfloat16)
        attended = finish_rows(
            part_recv[...],
            chip,
            q_group,
            nk_ref[...],
            nv_ref[...].astype(jnp.float32),
            sign_row,
            rotate,
            scale,
        )
        att[chip] = attended.astype(jnp.bfloat16).astype(jnp.float32)

        def send_att(o, _):
            remote(
                att.at[chip],
                att.at[chip],
                att_s.at[o],
                att_r.at[chip],
                lax.rem(me + o, INST),
                head,
            ).start()
            return 0

        lax.fori_loop(1, INST, send_att, 0)

    def att_from(c):
        return remote(att.at[c], att.at[c], att_s.at[0], att_r.at[c], 2 * c, head)

    def got_att(t, _):
        att_from(lax.rem(chip + t, 16)).wait_recv()
        return 0

    lax.fori_loop(1, 16, got_att, 0)

    @pl.when(core == 1)
    def _():
        att_from(chip).wait_recv()

    everyone = att[...]
    terms = jnp.zeros((16, 256), jnp.float32)
    for h in range(8):
        terms = terms + jnp.dot(
            everyone[:, h, :].astype(jnp.bfloat16),
            w_ref[h * HD : (h + 1) * HD, :],
            preferred_element_type=jnp.float32,
        )
    proj[head] = terms

    def proj_copy(o):
        return remote(
            proj.at[head],
            proj.at[head],
            proj_s.at[o],
            proj_r.at[head],
            me,
            lax.rem(head + o, HEADS),
        )

    def start_proj(o, _):
        proj_copy(o).start()
        return 0

    def got_proj(o, _):
        z = lax.rem(head + o, HEADS)
        remote(proj.at[z], proj.at[z], proj_s.at[o], proj_r.at[z], me, z).wait_recv()
        return 0

    lax.fori_loop(1, HEADS, start_proj, 0)
    lax.fori_loop(1, HEADS, got_proj, 0)
    out_ref[...] = jnp.sum(proj[...], axis=0)

    def sent_proj(o, _):
        proj_copy(o).wait_send()
        return 0

    def sent_part(t, _):
        part_copy(t).wait_send()
        return 0

    lax.fori_loop(1, HEADS, sent_proj, 0)
    lax.fori_loop(1, 16, sent_part, 0)

    @pl.when(core == 1)
    def _():
        part_copy(0).wait_send()

    @pl.when(core == 0)
    def _():
        def sent_att(o, _):
            remote(
                att.at[chip],
                att.at[chip],
                att_s.at[o],
                att_r.at[chip],
                lax.rem(me + o, INST),
                head,
            ).wait_send()
            return 0

        lax.fori_loop(1, INST, sent_att, 0)

    def moved(o, _):
        for copy in move(o):
            copy.wait_send()
        for copy in arrived(o):
            copy.wait_recv()
        return 0

    lax.fori_loop(1, INST, moved, 0)


def place_kernel(table_ref, proj_ref, rk_ref, rv_ref, out_ref, mk_ref, mv_ref, zeros, sems):
    zeros[...] = jnp.zeros_like(zeros)

    def place(s, _):
        row = table_ref[s]

        @pl.when(row >= 0)
        def _():
            pltpu.make_async_copy(rk_ref.at[row], mk_ref.at[s], sems.at[0]).start()
            pltpu.make_async_copy(rv_ref.at[row], mv_ref.at[s], sems.at[1]).start()

        @pl.when(row < 0)
        def _():
            pltpu.make_async_copy(zeros, mk_ref.at[s], sems.at[0]).start()
            pltpu.make_async_copy(zeros, mv_ref.at[s], sems.at[1]).start()

        return 0

    lax.fori_loop(0, SLOTS, place, 0)
    out_ref[...] = proj_ref[...].astype(jnp.bfloat16)
    pltpu.make_async_copy(rk_ref.at[pl.ds(0, SLOTS)], mk_ref, sems.at[0]).wait()
    pltpu.make_async_copy(rv_ref.at[pl.ds(0, SLOTS)], mv_ref, sems.at[1]).wait()


def move_tables(own, block_req, block_fill, dest_inst, new_slot):
    peers = jnp.arange(INST, dtype=jnp.int32)
    slots = jnp.arange(SLOTS, dtype=jnp.int32)
    ranks = jnp.arange(PER, dtype=jnp.int32)
    dest = dest_inst.reshape(INST, SLOTS)
    own_dest = lax.dynamic_index_in_dim(dest, own, 0, keepdims=False)
    same = (own_dest[:, None] == own_dest[None, :]) & (slots[None, :] < slots[:, None])
    own_rank = jnp.sum(same.astype(jnp.int32), axis=1)
    send = (
        (own_dest[None, None, :] == peers[:, None, None])
        & (own_rank[None, None, :] == ranks[None, :, None])
        & (own_dest[None, None, :] != own)
    )
    send_index = jnp.sum(jnp.where(send, slots[None, None, :], 0), axis=2).reshape(-1)
    to_me = (dest == own) & (peers[:, None] != own)
    rank = jnp.cumsum(to_me.astype(jnp.int32), axis=1) - 1
    row = jnp.where(to_me, peers[:, None] * PER + rank, -1).reshape(-1)
    lands = to_me.reshape(-1)[None, :] & (new_slot[None, :] == slots[:, None])
    table = jnp.max(jnp.where(lands, row[None, :], -1), axis=1)
    own_req = lax.dynamic_index_in_dim(block_req.reshape(INST, SLOTS), own, 0, keepdims=False)
    own_fill = lax.dynamic_index_in_dim(block_fill.reshape(INST, SLOTS), own, 0, keepdims=False)
    return jnp.concatenate([send_index, own_req, own_fill]), table


def shards(
    query,
    new_keys,
    new_values,
    cache_keys,
    cache_values,
    signs,
    block_req,
    block_fill,
    dest_inst,
    new_slot,
    out_weight,
):
    own = lax.axis_index("inst")
    plan, table = move_tables(own, block_req, block_fill, dest_inst, new_slot)
    vmem = pl.BlockSpec(memory_space=pltpu.VMEM)
    smem = pl.BlockSpec(memory_space=pltpu.SMEM)
    hbm = pl.BlockSpec(memory_space=pl.ANY)
    blocks = jax.ShapeDtypeStruct((INST, PER, BT, HD), jnp.bfloat16)
    dma = pltpu.SemaphoreType.DMA
    proj, got_keys, got_values = pl.pallas_call(
        layer_kernel,
        out_shape=(jax.ShapeDtypeStruct((16, 256), jnp.float32), blocks, blocks),
        in_specs=[smem, vmem, vmem, vmem, vmem, vmem, hbm, hbm],
        out_specs=(vmem, hbm, hbm),
        scratch_shapes=[
            pltpu.VMEM((SLOTS, BT, HD), jnp.bfloat16),
            pltpu.VMEM((SLOTS, BT, HD), jnp.bfloat16),
            pltpu.VMEM((INST, PER, BT, HD), jnp.bfloat16),
            pltpu.VMEM((INST, PER, BT, HD), jnp.bfloat16),
            pltpu.VMEM((SLOTS // CHUNK, ROWS, CHUNK * BT), jnp.float32),
            pltpu.VMEM((ROWS, HD), jnp.float32),
            pltpu.VMEM((16, 8, 2 * HD), jnp.float32),
            pltpu.VMEM((INST, 8, 2 * HD), jnp.float32),
            pltpu.VMEM((16, 8, HD), jnp.float32),
            pltpu.VMEM((HEADS, 16, 256), jnp.float32),
            dma((2,)),
            dma((INST,)),
            dma((INST,)),
            dma((INST,)),
            dma((INST,)),
            dma((16,)),
            dma((INST,)),
            dma((INST,)),
            dma((16,)),
            dma((HEADS,)),
            dma((HEADS,)),
        ],
        compiler_params=pltpu.CompilerParams(
            collective_id=0, has_side_effects=True, vmem_limit_bytes=48 * 2**20
        ),
    )(
        plan,
        query.reshape(ROWS, HD),
        new_keys.reshape(16, HD),
        new_values.reshape(16, HD),
        signs,
        out_weight,
        cache_keys.reshape(SLOTS, BT, HD),
        cache_values.reshape(SLOTS, BT, HD),
    )
    layer_out, moved_keys, moved_values = pl.pallas_call(
        place_kernel,
        out_shape=(
            jax.ShapeDtypeStruct((16, 256), jnp.bfloat16),
            jax.ShapeDtypeStruct((SLOTS, BT, HD), jnp.bfloat16),
            jax.ShapeDtypeStruct((SLOTS, BT, HD), jnp.bfloat16),
        ),
        in_specs=[smem, vmem, hbm, hbm],
        out_specs=(vmem, hbm, hbm),
        scratch_shapes=[pltpu.VMEM((BT, HD), jnp.bfloat16), dma((2,))],
    )(
        table,
        proj,
        got_keys.reshape(INST * PER, BT, HD),
        got_values.reshape(INST * PER, BT, HD),
    )
    return (
        layer_out.reshape(2, 8, 256),
        moved_keys.reshape(SLOTS, BT, 1, HD),
        moved_values.reshape(SLOTS, BT, 1, HD),
    )


def solution(mesh):
    placed = (
        P(None, None, "head", None),
        P(None, None, "head", None),
        P(None, None, "head", None),
        P("inst", None, "head", None),
        P("inst", None, "head", None),
        P("head", None),
        P(),
        P(),
        P(),
        P(),
        P("head", "inst"),
    )
    return jax.shard_map(
        shards,
        mesh=mesh,
        in_specs=placed,
        out_specs=(
            P(None, None, "inst"),
            P("inst", None, "head", None),
            P("inst", None, "head", None),
        ),
        check_vma=False,
    )
```

time: 290 us -> 360 us (1.24)
  the two profiles are of different devices: /device:TPU:8 before, /device:TPU:1 now
where the time goes in v1:
time: 360 us; the launch traced here: 359 us
  Pallas kernels  345 us (96%)
  local copies, waits for them, and re-layouts  10.3 us (3%)
    pallas_call x1, Pallas kernels, shards(): pl.pallas_call(layer_kernel, out_shape=(jax.ShapeDtypeStruct((16, 256), j...  216 us
    pallas_call x1, Pallas kernels, shards(): pl.pallas_call(place_kernel, out_shape=(jax.ShapeDtypeStruct((16, 256), j...  130 us
    unnamed x16, local copies, waits for them, and re-layouts  7.6 us

profile of v1, /device:TPU:1, one launch (start us, length us, event | category | flops | bytes accessed | tf_op | source)
XLA Modules:
  0.0 359.1 jit_solution(3054614216685624295)
XLA Ops:
  0.7 0.1 and.48
  0.7 0.1 and.49
  0.8 0.8 reshape.142
  1.6 0.1 and_convert_fusion
  1.7 0.2 reduce_window_sum.11
  1.9 0.1 add_add_fusion
  2.0 0.1 add.25
  2.0 0.7 broadcast_select_fusion
  2.8 1.5 select_reduce_fusion.table_ref
  4.2 0.2 convert_reduce_fusion
  4.4 0.2 select_reduce_fusion.1
  4.6 0.1 copy.18
  4.7 0.1 reshape.143
  4.8 0.8 reshape.144
  5.5 0.8 reshape.145
  6.3 0.1 pad_add_fusion.plan_ref
  6.4 0.0 copy-start
  6.4 1.6 copy-done
  8.0 0.0 copy-start.1
  8.0 1.6 copy-done.1
  9.6 0.0 copy-start.2
  9.6 1.0 copy-done.2
  10.6 0.0 copy-start.3
  10.6 0.8 copy-done.3
  11.4 0.0 copy-start.5
  11.4 0.7 copy-done.5
  12.1 0.0 copy-start.6
  12.1 0.7 copy-done.6
  12.8 0.0 copy-start.7
  12.8 0.7 copy-done.7
  13.4 215.6 %shard_map.130 = (f32[16,256]{1,0:T(8,128)S(1)}, bf16[32,4,128,128]{3,2,1,0:T(8,128)(2,1)}, bf16[32,4,128,128]{3,2,1,0:T(8,128)(2,1)}) custom-call(s32[256]{0:T(256)S(1)} %pad_add_fusion.plan_ref, bf16[128,128]{1,0:T(8,128)(2,1)S(1)} %bitcast.23, bf16[16,128]{1,0:T(8,128)(2,1)S(1)} %bitcast.24, bf16[16,128]{1,0:T(8,128)(2,1)S(1)} %bitcast.25, ...), custom_call_target="tpu_custom_call" | custom-call | tf_op jit(solution)/shard_map/pallas_call | solution.py:424
  229.0 0.0 copy-start.4
  229.0 0.6 copy-done.4
  229.6 129.5 %shard_map.131 = (bf16[16,256]{1,0:T(8,128)(2,1)}, bf16[64,128,128]{2,1,0:T(8,128)(2,1)}, bf16[64,128,128]{2,1,0:T(8,128)(2,1)}) custom-call(s32[64]{0:T(128)} %select_reduce_fusion.table_ref, f32[16,256]{1,0:T(8,128)} %copy-done.4, bf16[128,128,128]{2,1,0:T(8,128)(2,1)} %bitcast.26, bf16[128,128,128]{2,1,0:T(8,128)(2,1)} %bitcast.27), custom_call_target="tpu_custom_call" | custom-call | tf_op jit(solution)/shard_map/pallas_call | solution.py:465
  (6 shorter events, 0.0 us)
Async XLA Ops:
  6.4 1.6 copy-start
  8.0 1.6 copy-start.1
  9.6 1.0 copy-start.2
  10.6 0.8 copy-start.3
  11.4 0.7 copy-start.5
  12.1 0.7 copy-start.6
  12.8 0.7 copy-start.7
  229.0 0.6 copy-start.4

commit v2 on v1

--- a/solution.py
+++ b/solution.py
@@ -3,6 +3,7 @@
 
 import jax
 import jax.numpy as jnp
+import numpy as np
 from jax import lax
 from jax.experimental import pallas as pl
 from jax.experimental.pallas import tpu as pltpu
@@ -19,6 +20,10 @@
 HD = 128
 ROWS = 128
 CHUNK = 4
+GROUP = 8
+SPLITS = (((0, 1), (2, 3)), ((0, 2), (1, 3)), ((0, 3), (1, 2)))
+VARIANTS = ((0, 6, 6), (0, 8, 8))
+T_U, T_V, SRC_K, DST_K, SRC_V, DST_V, REQ, FILL, PLAN = 0, 128, 256, 264, 272, 280, 288, 352, 416
 
 
 def hadamard(order_size):
@@ -54,8 +59,8 @@
             q_low, keys, (((1,), (1,)), ((), ())), preferred_element_type=jnp.float32
         )
         for c in range(CHUNK):
-            req = plan_ref[128 + i * CHUNK + c]
-            fill = plan_ref[192 + i * CHUNK + c]
+            req = plan_ref[REQ + i * CHUNK + c]
+            fill = plan_ref[FILL + i * CHUNK + c]
             live = (row_req == req) & (token < fill)
             part = jnp.where(live, s[:, c * BT : (c + 1) * BT] * scale, NEG_FILL)
             scores[i, :, c * BT : (c + 1) * BT] = part
@@ -106,44 +111,74 @@
     return (back + fresh) / denominator
 
 
-def layer_kernel(
-    plan_ref,
-    q_ref,
-    nk_ref,
-    nv_ref,
-    signs_ref,
-    w_ref,
-    ck_ref,
-    cv_ref,
-    out_ref,
-    rk_ref,
-    rv_ref,
-    kc,
-    vc,
-    sk,
-    sv,
-    scores,
-    qf,
-    part_send,
-    part_recv,
-    att,
-    proj,
-    load_sem,
-    k_send,
-    k_recv,
-    v_send,
-    v_recv,
-    part_s,
-    part_r,
-    att_s,
-    att_r,
-    proj_s,
-    proj_r,
-):
+def coordinates(inst, split):
+    x, y = inst // 8, inst // 2 % 4
+    code = jnp.bitwise_xor(x, x // 2) + 4 * jnp.bitwise_xor(y, y // 2)
+    (a0, a1), (b0, b1) = SPLITS[split]
+
+    def bit(b):
+        return code // (1 << b) % 2
+
+    return bit(a0) + 2 * bit(a1), bit(b0) + 2 * bit(b1), inst % 2
+
+
+def instance(u, v, core, split):
+    (a0, a1), (b0, b1) = SPLITS[split]
+    code = (u % 2) * (1 << a0) + (u // 2) * (1 << a1) + (v % 2) * (1 << b0) + (v // 2) * (1 << b1)
+    gx, gy = code % 4, code // 4
+    return jnp.bitwise_xor(gx, gx // 2) * 8 + jnp.bitwise_xor(gy, gy // 2) * 2 + core
+
+
+def layer_kernel(split, cap1, cap2, *refs):
+    (
+        plan_ref,
+        q_ref,
+        nk_ref,
+        nv_ref,
+        signs_ref,
+        w_ref,
+        ck_ref,
+        cv_ref,
+        out_ref,
+        rk_ref,
+        rv_ref,
+        kc,
+        vc,
+        first_send,
+        mid_k0,
+        mid_k1,
+        mid_v0,
+        mid_v1,
+        second_send,
+        scores,
+        qf,
+        part_send,
+        part_recv,
+        att,
+        proj,
+        load_sem,
+        first_s,
+        first_r,
+        second_s,
+        second_r,
+        part_s,
+        part_r,
+        att_s,
+        att_r,
+        proj_s,
+        proj_r,
+    ) = refs
     me = lax.axis_index("inst")
     head = lax.axis_index("head")
     chip, core = me // 2, me % 2
+    u, v, _ = coordinates(me, split)
     scale = 1.0 / math.sqrt(HD)
+    caches = (kc, vc)
+    mids = ((mid_k0, mid_k1), (mid_v0, mid_v1))
+    lands = (rk_ref, rv_ref)
+    tables = (T_U, T_V)
+    sources = (SRC_K, SRC_V)
+    dests = (DST_K, DST_V)
 
     load_k = pltpu.make_async_copy(ck_ref, kc, load_sem.at[0])
     load_v = pltpu.make_async_copy(cv_ref, vc, load_sem.at[1])
@@ -182,31 +217,96 @@
     load_v.wait()
     pl.semaphore_wait(barrier, INST - 1 + HEADS - 1)
 
-    def move(o):
-        to = lax.rem(me + o, INST)
-        return (
-            remote(sk.at[o], rk_ref.at[me], k_send.at[o], k_recv.at[me], to, head),
-            remote(sv.at[o], rv_ref.at[me], v_send.at[o], v_recv.at[me], to, head),
-        )
-
-    def arrived(o):
-        src = lax.rem(me + o, INST)
-        return (
-            remote(sk.at[o], rk_ref.at[src], k_send.at[o], k_recv.at[src], src, head),
-            remote(sv.at[o], rv_ref.at[src], v_send.at[o], v_recv.at[src], src, head),
-        )
-
-    def send_blocks(o, _):
-        to = lax.rem(me + o, INST)
-        for k in range(PER):
-            b = plan_ref[to * PER + k]
-            sk[o, k] = kc[b]
-            sv[o, k] = vc[b]
-        for copy in move(o):
-            copy.start()
-        return 0
-
-    lax.fori_loop(1, INST, send_blocks, 0)
+    def peer(plane, along_first, d, j):
+        if (plane == 0) == along_first:
+            return instance(jnp.bitwise_xor(u, d), v, j, split)
+        return instance(u, jnp.bitwise_xor(v, d), j, split)
+
+    def first_copy(plane, half, d, j):
+        src = first_send.at[plane, half, d * 2 + j]
+        dst = mids[plane][half].at[pl.ds((d * 2 + core) * GROUP, cap1)]
+        sems = first_s.at[plane, half, d * 2 + j], first_r.at[plane, half, d * 2 + core]
+        return remote(src, dst, *sems, peer(plane, True, d, j), head)
+
+    def first_keep(plane, half):
+        return pltpu.make_async_copy(
+            first_send.at[plane, half, core],
+            mids[plane][half].at[pl.ds(core * GROUP, cap1)],
+            first_r.at[plane, half, core],
+        )
+
+    def first_wait(plane, half, d, j):
+        dst = mids[plane][half].at[pl.ds((d * 2 + j) * GROUP, cap1)]
+        return pltpu.make_async_copy(dst, dst, first_r.at[plane, half, d * 2 + j])
+
+    def second_copy(plane, half, d, j):
+        src = second_send.at[plane, half, d * 2 + j]
+        dst = lands[plane].at[pl.ds((half * 8 + d * 2 + core) * GROUP, cap2)]
+        sems = second_s.at[plane, half, d * 2 + j], second_r.at[plane, half, d * 2 + core]
+        return remote(src, dst, *sems, peer(plane, False, d, j), head)
+
+    def second_keep(plane, half):
+        return pltpu.make_async_copy(
+            second_send.at[plane, half, core],
+            lands[plane].at[pl.ds((half * 8 + core) * GROUP, cap2)],
+            second_r.at[plane, half, core],
+        )
+
+    def second_wait(plane, half, d, j):
+        dst = lands[plane].at[pl.ds((half * 8 + d * 2 + j) * GROUP, cap2)]
+        return pltpu.make_async_copy(dst, dst, second_r.at[plane, half, d * 2 + j])
+
+    def start_first(half):
+        def body(t, _):
+            d, j = 3 - t // 2, t % 2
+            for plane in range(2):
+                first = jnp.bitwise_xor(u if plane == 0 else v, d)
+                for m in range(cap1):
+                    b = plan_ref[tables[plane] + first * 32 + m * PER + j * 2 + half]
+                    first_send[plane, half, d * 2 + j, m] = caches[plane][b]
+
+                @pl.when((d > 0) | (j != core))
+                def _(plane=plane):
+                    first_copy(plane, half, d, j).start()
+
+                @pl.when((d == 0) & (j == core))
+                def _(plane=plane):
+                    first_keep(plane, half).start()
+
+            return 0
+
+        lax.fori_loop(0, 8, body, 0)
+
+    def start_second(half):
+        def wait_body(t, _):
+            for plane in range(2):
+                first_wait(plane, half, t // 2, t % 2).wait()
+            return 0
+
+        lax.fori_loop(0, 8, wait_body, 0)
+
+        def body(t, _):
+            d, j = 3 - t // 2, t % 2
+            for plane in range(2):
+                base = plan_ref[dests[plane] + d * 2 + j]
+                for n in range(cap2):
+                    b = base + plan_ref[sources[plane] + n]
+                    second_send[plane, half, d * 2 + j, n] = mids[plane][half][b]
+
+                @pl.when((d > 0) | (j != core))
+                def _(plane=plane):
+                    second_copy(plane, half, d, j).start()
+
+                @pl.when((d == 0) & (j == core))
+                def _(plane=plane):
+                    second_keep(plane, half).start()
+
+            return 0
+
+        lax.fori_loop(0, 8, body, 0)
+
+    start_first(0)
+    start_first(1)
 
     row_max, row_total, acc = attend(plan_ref, q_low, kc, vc, scores, scale)
     lane = lax.broadcasted_iota(jnp.int32, (ROWS, HD), 1)
@@ -228,6 +328,8 @@
     @pl.when(core == 1)
     def _():
         part_copy(0).start()
+
+    start_second(0)
 
     @pl.when(core == 0)
     def _():
@@ -266,6 +368,8 @@
             return 0
 
         lax.fori_loop(1, INST, send_att, 0)
+
+    start_second(1)
 
     def att_from(c):
         return remote(att.at[c], att.at[c], att_s.at[0], att_r.at[c], 2 * c, head)
@@ -343,62 +447,198 @@
 
         lax.fori_loop(1, INST, sent_att, 0)
 
-    def moved(o, _):
-        for copy in move(o):
-            copy.wait_send()
-        for copy in arrived(o):
-            copy.wait_recv()
-        return 0
-
-    lax.fori_loop(1, INST, moved, 0)
-
-
-def place_kernel(table_ref, proj_ref, rk_ref, rv_ref, out_ref, mk_ref, mv_ref, zeros, sems):
-    zeros[...] = jnp.zeros_like(zeros)
+    def finish(t, _):
+        d, j = t // 2, t % 2
+        for half in range(2):
+            for plane in range(2):
+
+                @pl.when((d > 0) | (j != core))
+                def _(plane=plane, half=half):
+                    first_copy(plane, half, d, j).wait_send()
+                    second_copy(plane, half, d, j).wait_send()
+
+                second_wait(plane, half, d, j).wait()
+        return 0
+
+    lax.fori_loop(0, 8, finish, 0)
+
+
+def layer_call(variant, operands):
+    split, cap1, cap2 = VARIANTS[variant]
+    vmem = pl.BlockSpec(memory_space=pltpu.VMEM)
+    smem = pl.BlockSpec(memory_space=pltpu.SMEM)
+    hbm = pl.BlockSpec(memory_space=pl.ANY)
+    blocks = jax.ShapeDtypeStruct((2 * 8 * GROUP, BT, HD), jnp.bfloat16)
+    dma = pltpu.SemaphoreType.DMA
+
+    def low(*lead):
+        return pltpu.VMEM((*lead, BT, HD), jnp.bfloat16)
+
+    return pl.pallas_call(
+        functools.partial(layer_kernel, split, cap1, cap2),
+        out_shape=(jax.ShapeDtypeStruct((16, 256), jnp.float32), blocks, blocks),
+        in_specs=[smem, vmem, vmem, vmem, vmem, vmem, hbm, hbm],
+        out_specs=(vmem, hbm, hbm),
+        scratch_shapes=[
+            low(SLOTS),
+            low(SLOTS),
+            low(2, 2, 8, cap1),
+            low(8 * GROUP),
+            low(8 * GROUP),
+            low(8 * GROUP),
+            low(8 * GROUP),
+            low(2, 2, 8, cap2),
+            pltpu.VMEM((SLOTS // CHUNK, ROWS, CHUNK * BT), jnp.float32),
+            pltpu.VMEM((ROWS, HD), jnp.float32),
+            pltpu.VMEM((16, 8, 2 * HD), jnp.float32),
+            pltpu.VMEM((INST, 8, 2 * HD), jnp.float32),
+            pltpu.VMEM((16, 8, HD), jnp.float32),
+            pltpu.VMEM((HEADS, 16, 256), jnp.float32),
+            dma((2,)),
+            dma((2, 2, 8)),
+            dma((2, 2, 8)),
+            dma((2, 2, 8)),
+            dma((2, 2, 8)),
+            dma((16,)),
+            dma((INST,)),
+            dma((INST,)),
+            dma((16,)),
+            dma((HEADS,)),
+            dma((HEADS,)),
+        ],
+        compiler_params=pltpu.CompilerParams(
+            collective_id=variant, has_side_effects=True, vmem_limit_bytes=56 * 2**20
+        ),
+    )(*operands)
+
+
+def place_kernel(table_ref, proj_ref, rk_ref, rv_ref, out_ref, mk_ref, mv_ref, sems):
+    lands = ((rk_ref, mk_ref), (rv_ref, mv_ref))
 
     def place(s, _):
-        row = table_ref[s]
-
-        @pl.when(row >= 0)
-        def _():
-            pltpu.make_async_copy(rk_ref.at[row], mk_ref.at[s], sems.at[0]).start()
-            pltpu.make_async_copy(rv_ref.at[row], mv_ref.at[s], sems.at[1]).start()
-
-        @pl.when(row < 0)
-        def _():
-            pltpu.make_async_copy(zeros, mk_ref.at[s], sems.at[0]).start()
-            pltpu.make_async_copy(zeros, mv_ref.at[s], sems.at[1]).start()
+        for plane, (src, dst) in enumerate(lands):
+            row = table_ref[plane * SLOTS + s]
+
+            @pl.when(row >= 0)
+            def _(plane=plane, src=src, dst=dst, row=row):
+                pltpu.make_async_copy(src.at[row], dst.at[s], sems.at[plane]).start()
+
+            @pl.when(row < 0)
+            def _(dst=dst):
+                dst[s] = jnp.zeros((BT, HD), jnp.bfloat16)
 
         return 0
 
     lax.fori_loop(0, SLOTS, place, 0)
     out_ref[...] = proj_ref[...].astype(jnp.bfloat16)
-    pltpu.make_async_copy(rk_ref.at[pl.ds(0, SLOTS)], mk_ref, sems.at[0]).wait()
-    pltpu.make_async_copy(rv_ref.at[pl.ds(0, SLOTS)], mv_ref, sems.at[1]).wait()
-
-
-def move_tables(own, block_req, block_fill, dest_inst, new_slot):
-    peers = jnp.arange(INST, dtype=jnp.int32)
-    slots = jnp.arange(SLOTS, dtype=jnp.int32)
-    ranks = jnp.arange(PER, dtype=jnp.int32)
+
+    def settle(s, _):
+        for plane, (src, dst) in enumerate(lands):
+            row = table_ref[plane * SLOTS + s]
+
+            @pl.when(row >= 0)
+            def _(plane=plane, src=src, dst=dst, row=row):
+                pltpu.make_async_copy(src.at[row], dst.at[s], sems.at[plane]).wait()
+
+        return 0
+
+    lax.fori_loop(0, SLOTS, settle, 0)
+
+
+def static_groups():
+    out = []
+    for (a0, a1), (b0, b1) in SPLITS:
+        rows = []
+        for inst in range(INST):
+            x, y = inst // 8, inst // 2 % 4
+            code = (x ^ (x // 2)) + 4 * (y ^ (y // 2))
+            bits = [code >> b & 1 for b in range(4)]
+            rows.append((bits[a0] + 2 * bits[a1], bits[b0] + 2 * bits[b1]))
+        out.append(np.array(rows, np.int32).T)
+    return np.stack(out)
+
+
+def move_plan(own, block_req, block_fill, dest_inst, new_slot):
+    i32 = jnp.int32
+    peers = jnp.arange(INST, dtype=i32)
+    slots = jnp.arange(SLOTS, dtype=i32)
     dest = dest_inst.reshape(INST, SLOTS)
-    own_dest = lax.dynamic_index_in_dim(dest, own, 0, keepdims=False)
-    same = (own_dest[:, None] == own_dest[None, :]) & (slots[None, :] < slots[:, None])
-    own_rank = jnp.sum(same.astype(jnp.int32), axis=1)
-    send = (
-        (own_dest[None, None, :] == peers[:, None, None])
-        & (own_rank[None, None, :] == ranks[None, :, None])
-        & (own_dest[None, None, :] != own)
-    )
-    send_index = jnp.sum(jnp.where(send, slots[None, None, :], 0), axis=2).reshape(-1)
-    to_me = (dest == own) & (peers[:, None] != own)
-    rank = jnp.cumsum(to_me.astype(jnp.int32), axis=1) - 1
-    row = jnp.where(to_me, peers[:, None] * PER + rank, -1).reshape(-1)
-    lands = to_me.reshape(-1)[None, :] & (new_slot[None, :] == slots[:, None])
-    table = jnp.max(jnp.where(lands, row[None, :], -1), axis=1)
-    own_req = lax.dynamic_index_in_dim(block_req.reshape(INST, SLOTS), own, 0, keepdims=False)
-    own_fill = lax.dynamic_index_in_dim(block_fill.reshape(INST, SLOTS), own, 0, keepdims=False)
-    return jnp.concatenate([send_index, own_req, own_fill]), table
+    slot_of = new_slot.reshape(INST, SLOTS)
+    released = dest[:, 0] != peers
+    groups = static_groups()
+
+    def needs(split):
+        u, v = jnp.asarray(groups[split])
+        most_kept, most_gone = jnp.zeros((), i32), jnp.zeros((), i32)
+        for coord in (u, v):
+            inside = coord[None, :] == jnp.arange(4, dtype=i32)[:, None]
+            gone = jnp.sum((inside & released[None, :]).astype(i32), axis=1)
+            most_gone = jnp.maximum(most_gone, jnp.max(gone))
+            most_kept = jnp.maximum(most_kept, 8 - jnp.min(gone))
+        return most_kept, most_gone
+
+    need = {split: needs(split) for split in sorted({variant[0] for variant in VARIANTS})}
+    choice = jnp.full((), len(VARIANTS) - 1, i32)
+    for index in reversed(range(len(VARIANTS) - 1)):
+        split, cap1, cap2 = VARIANTS[index]
+        fits = (need[split][0] <= cap1) & (need[split][1] <= cap2)
+        choice = jnp.where(fits, index, choice)
+    used = [split for split, _, _ in VARIANTS]
+    coords = jnp.asarray(groups[used[-1]])
+    for index in range(len(VARIANTS) - 1):
+        if used[index] != used[-1]:
+            coords = jnp.where(choice == index, jnp.asarray(groups[used[index]]), coords)
+    core = peers % 2
+    mine = (peers == own).astype(i32)
+    before = peers[None, :] < peers[:, None]
+    own_dest = jnp.sum(dest * mine[:, None], axis=0)
+    own_rank = jnp.sum(
+        ((own_dest[:, None] == own_dest[None, :]) & (slots[None, :] < slots[:, None])).astype(i32),
+        axis=1,
+    )
+    to_me = (dest == own) & released[:, None]
+    rank = jnp.sum(
+        (to_me[:, None, :] & (slots[None, None, :] < slots[None, :, None])).astype(i32), axis=2
+    )
+    sends, extras, rows = [], [], []
+    for plane in range(2):
+        first, second = (coords[0], coords[1]) if plane == 0 else (coords[1], coords[0])
+        own_first, own_second = jnp.sum(first * mine), jnp.sum(second * mine)
+        kept_rank = jnp.sum(
+            ((first[:, None] == first[None, :]) & before & ~released[None, :]).astype(i32), axis=1
+        )
+        gone_rank = jnp.sum(
+            ((second[:, None] == second[None, :]) & before & released[None, :]).astype(i32), axis=1
+        )
+        place = first * 32 + kept_rank * PER
+        sent = jnp.sum(
+            jnp.where(own_dest[:, None] == peers[None, :], place[None, :], 0), axis=1
+        )
+        at = sent + own_rank
+        hit = at[None, :] == jnp.arange(128, dtype=i32)[:, None]
+        sends.append(jnp.sum(jnp.where(hit, slots[None, :], 0), axis=1))
+        lane = jnp.arange(8, dtype=i32)[:, None]
+        source = (jnp.bitwise_xor(first, own_first) * 2 + core) * GROUP
+        take = released & (second == own_second)
+        extras.append(
+            jnp.sum(jnp.where(take[None, :] & (gone_rank[None, :] == lane), source[None, :], 0), 1)
+        )
+        distance = jnp.bitwise_xor(second, own_second) * 2 + core
+        take = first == own_first
+        extras.append(
+            jnp.sum(jnp.where(take[None, :] & (distance[None, :] == lane), kept_rank[None, :], 0), 1)
+        )
+        base = jnp.bitwise_xor(second, own_second) * 2 * GROUP + gone_rank
+        rows.append(
+            base[:, None] + (rank // 2) * GROUP + (rank % 2) * 8 * GROUP
+        )
+    lands = to_me[None] & (slot_of[None] == slots[:, None, None])
+    table = [
+        jnp.max(jnp.where(lands, row[None], -1), axis=(1, 2)) for row in rows
+    ]
+    own_req = jnp.sum(block_req.reshape(INST, SLOTS) * mine[:, None], axis=0)
+    own_fill = jnp.sum(block_fill.reshape(INST, SLOTS) * mine[:, None], axis=0)
+    return choice, jnp.concatenate([*sends, *extras, own_req, own_fill]), jnp.concatenate(table)
 
 
 def shards(
@@ -415,44 +655,8 @@
     out_weight,
 ):
     own = lax.axis_index("inst")
-    plan, table = move_tables(own, block_req, block_fill, dest_inst, new_slot)
-    vmem = pl.BlockSpec(memory_space=pltpu.VMEM)
-    smem = pl.BlockSpec(memory_space=pltpu.SMEM)
-    hbm = pl.BlockSpec(memory_space=pl.ANY)
-    blocks = jax.ShapeDtypeStruct((INST, PER, BT, HD), jnp.bfloat16)
-    dma = pltpu.SemaphoreType.DMA
-    proj, got_keys, got_values = pl.pallas_call(
-        layer_kernel,
-        out_shape=(jax.ShapeDtypeStruct((16, 256), jnp.float32), blocks, blocks),
-        in_specs=[smem, vmem, vmem, vmem, vmem, vmem, hbm, hbm],
-        out_specs=(vmem, hbm, hbm),
-        scratch_shapes=[
-            pltpu.VMEM((SLOTS, BT, HD), jnp.bfloat16),
-            pltpu.VMEM((SLOTS, BT, HD), jnp.bfloat16),
-            pltpu.VMEM((INST, PER, BT, HD), jnp.bfloat16),
-            pltpu.VMEM((INST, PER, BT, HD), jnp.bfloat16),
-            pltpu.VMEM((SLOTS // CHUNK, ROWS, CHUNK * BT), jnp.float32),
-            pltpu.VMEM((ROWS, HD), jnp.float32),
-            pltpu.VMEM((16, 8, 2 * HD), jnp.float32),
-            pltpu.VMEM((INST, 8, 2 * HD), jnp.float32),
-            pltpu.VMEM((16, 8, HD), jnp.float32),
-            pltpu.VMEM((HEADS, 16, 256), jnp.float32),
-            dma((2,)),
-            dma((INST,)),
-            dma((INST,)),
-            dma((INST,)),
-            dma((INST,)),
-            dma((16,)),
-            dma((INST,)),
-            dma((INST,)),
-            dma((16,)),
-            dma((HEADS,)),
-            dma((HEADS,)),
-        ],
-        compiler_params=pltpu.CompilerParams(
-            collective_id=0, has_side_effects=True, vmem_limit_bytes=48 * 2**20
-        ),
-    )(
+    choice, plan, table = move_plan(own, block_req, block_fill, dest_inst, new_slot)
+    operands = (
         plan,
         query.reshape(ROWS, HD),
         new_keys.reshape(16, HD),
@@ -462,6 +666,11 @@
         cache_keys.reshape(SLOTS, BT, HD),
         cache_values.reshape(SLOTS, BT, HD),
     )
+    branches = [functools.partial(layer_call, variant) for variant in range(len(VARIANTS))]
+    proj, got_keys, got_values = lax.switch(choice, branches, operands)
+    vmem = pl.BlockSpec(memory_space=pltpu.VMEM)
+    smem = pl.BlockSpec(memory_space=pltpu.SMEM)
+    hbm = pl.BlockSpec(memory_space=pl.ANY)
     layer_out, moved_keys, moved_values = pl.pallas_call(
         place_kernel,
         out_shape=(
@@ -470,14 +679,10 @@
             jax.ShapeDtypeStruct((SLOTS, BT, HD), jnp.bfloat16),
         ),
         in_specs=[smem, vmem, hbm, hbm],
-        out_specs=(vmem, hbm, hbm),
-        scratch_shapes=[pltpu.VMEM((BT, HD), jnp.bfloat16), dma((2,))],
-    )(
-        table,
-        proj,
-        got_keys.reshape(INST * PER, BT, HD),
-        got_values.reshape(INST * PER, BT, HD),
-    )
+        out_specs=(vmem, vmem, vmem),
+        scratch_shapes=[pltpu.SemaphoreType.DMA((2,))],
+        compiler_params=pltpu.CompilerParams(vmem_limit_bytes=32 * 2**20),
+    )(table, proj, got_keys, got_values)
     return (
         layer_out.reshape(2, 8, 256),
         moved_keys.reshape(SLOTS, BT, 1, HD),

time: 360 us -> 137 us (0.38)
  Pallas kernels: 345 us -> 113 us
  other arithmetic: 2.97 us -> 16.6 us
  local copies, waits for them, and re-layouts: 10.3 us -> 3.27 us
    pallas_call x1, Pallas kernels: 130 us -> 5.06 us  [shards(): pl.pallas_call(place_kernel, out_shape=(jax.ShapeDtypeStruct((16, 256), j...]
    pallas_call x1, Pallas kernels: 216 us -> 108 us  [layer_call(): pl.pallas_call(functools.partial(layer_kernel, split, cap1, cap2), out_sh...]
    unnamed x16 -> x0, local copies, waits for them, and re-layouts: 7.6 us -> none
    reduce_sum x2 -> x12, other arithmetic: 0.33 us -> 5.84 us  [the longest x2 2.59 us: move_plan(): own_first, own_second = (jnp.sum(first * mine), jnp.sum(second * mine))]
where the time goes in v2:
time: 137 us; the launch traced here: 136 us
  Pallas kernels  113 us (82%)
  other arithmetic  16.6 us (12%)
  local copies, waits for them, and re-layouts  3.27 us (2%)
  between operations  3.24 us (2%)
    pallas_call x1, Pallas kernels, layer_call(): pl.pallas_call(functools.partial(layer_kernel, split, cap1, cap2), out_sh...  108 us
    pallas_call x1, Pallas kernels, shards(): pl.pallas_call(place_kernel, out_shape=(jax.ShapeDtypeStruct((16, 256), j...  5.06 us

profile of v2, /device:TPU:1, one launch (start us, length us, event | category | flops | bytes accessed | tf_op | source)
XLA Modules:
  0.0 136.0 jit_solution(10739779151287932370)
XLA Ops:
  0.6 1.3 select_reduce_fusion.10
  1.9 1.3 select_reduce_fusion.11
  3.2 1.3 multiply_bitcast_fusion
  4.5 1.3 fusion.17
  5.9 0.8 reshape.264
  6.6 0.1 slice_reduce_fusion
  6.7 0.1 fusion.5
  6.9 0.8 convert_reduce_fusion.6
  7.7 0.7 fusion.20
  11.0 1.0 convert_reduce_fusion.2
  11.9 0.7 multiply_add_fusion.2
  12.6 2.0 %multiply_add_fusion.4 = (s32[32]{0:T(128)S(1)}, s32[32]{0:T(128)S(1)}) fusion(s32[32]{0:T(128)S(1)} %get-tuple-element.84, s32[32]{0:T(128)} %constant.82, s32[]{:T(128)} %select_reduce_fusion.10, s32[32]{0:T(128)S(1)} %get-tuple-element.85, s32[32]{0:T(128)} %constant.80, s32[]{:T(128)} %select_reduce_fusion.11), kind=kLoop, calls=%fused_computation.73 | loop fusion | flops 192 | bytes 776 | tf_op jit(solution)/shard_map/add | solution.py:631
  14.6 2.0 %compare_bitcast_fusion.1 = (pred[32]{0:T(512)(128)(4,1)S(1)}, pred[32]{0:T(512)(128)(4,1)S(1)}, pred[32]{0:T(512)(128)(4,1)S(1)}, pred[32]{0:T(512)(128)(4,1)S(1)}) fusion(s32[1,32]{1,0:T(1,128)} %constant.79, s32[]{:T(128)} %select_reduce_fusion.11, s32[32]{0:T(128)S(1)} %slice_reduce_fusion, s32[1,32]{1,0:T(1,128)} %constant.81, s32[]{:T(128)} %select_reduce_fusion.10), kind=kLoop, calls=%fused_computation.54 | loop fusion | flops 160 | bytes 520 | tf_op jit(solution)/shard_map/and | solution.py:629
  16.5 0.1 select_reduce_fusion.8
  16.7 0.2 select_reduce_fusion.6
  16.9 0.1 compare_and_fusion
  16.9 0.6 convert_reduce_fusion
  17.6 0.1 add_add_fusion
  17.6 0.8 reshape.265
  18.4 0.8 reshape.266
  19.2 0.1 multiply_reduce_fusion
  19.3 0.1 select_reduce_fusion.4
  19.4 0.2 convert_reduce_fusion.1
  19.6 0.1 select_reduce_fusion.2
  19.6 0.1 select_reduce_fusion.3
  19.7 0.1 concatenate.7
  19.8 0.8 eq.123
  20.6 2.4 %select_reduce_fusion.1 = (s32[64]{0:T(128)S(1)}, s32[64]{0:T(128)S(1)}) fusion(s32[32,64]{1,0:T(8,128)S(1)} %get-tuple-element.93, s32[32,64]{1,0:T(8,128)S(1)} %eq.123, pred[32,64]{1,0:T(8,128)(4,1)S(1)} %compare_and_fusion, s32[32,64]{1,0:T(8,128)S(1)} %get-tuple-element.92), kind=kLoop, calls=%fused_computation.1 | loop fusion | flops 786304 | bytes 27136 | tf_op jit(solution)/shard_map/reduce_max | solution.py:637
  23.0 0.1 pad_add_fusion.table_ref
  23.1 107.9 %conditional.1 = ((f32[16,256]{1,0:T(8,128)S(1)}, bf16[128,128,128]{2,1,0:T(8,128)(2,1)}, bf16[128,128,128]{2,1,0:T(8,128)(2,1)})) conditional(s32[]{:T(128)} %clamp.3, (s32[416]{0:T(512)S(1)}, bf16[128,128]{1,0:T(8,128)(2,1)}, bf16[16,128]{1,0:T(8,128)(2,1)}, bf16[16,128]{1,0:T(8,128)(2,1)}, s32[1,128]{1,0:T(1,128)}, ...), branch_computations={%region_27.28_spmd, %region_28.29_spmd} | conditional | bytes 8 | solution.py:670
  23.1 107.9 %branch_1_fun.1 = (f32[16,256]{1,0:T(8,128)S(1)}, bf16[128,128,128]{2,1,0:T(8,128)(2,1)}, bf16[128,128,128]{2,1,0:T(8,128)(2,1)}) custom-call(s32[416]{0:T(512)S(1)} %get-tuple-element.40.refs_0_, bf16[128,128]{1,0:T(8,128)(2,1)} %get-tuple-element.41.refs_1_, bf16[16,128]{1,0:T(8,128)(2,1)} %get-tuple-element.42.refs_2_, ...), custom_call_target="tpu_custom_call" | custom-call | tf_op jit(solution)/shard_map/cond/branch_1_fun/pallas_call | solution.py:477
  131.0 5.1 %shard_map.148 = (bf16[16,256]{1,0:T(8,128)(2,1)}, bf16[64,128,128]{2,1,0:T(8,128)(2,1)}, bf16[64,128,128]{2,1,0:T(8,128)(2,1)}) custom-call(s32[128]{0:T(128)S(1)} %pad_add_fusion.table_ref, f32[16,256]{1,0:T(8,128)S(1)} %get-tuple-element.57.proj_ref, bf16[128,128,128]{2,1,0:T(8,128)(2,1)} %get-tuple-element.58.rk_ref, ...), custom_call_target="tpu_custom_call" | custom-call | tf_op jit(solution)/shard_map/pallas_call | solution.py:674
  (4 shorter events, 0.0 us)

commit v3 on v2

--- a/solution.py
+++ b/solution.py
@@ -22,8 +22,23 @@
 CHUNK = 4
 GROUP = 8
 SPLITS = (((0, 1), (2, 3)), ((0, 2), (1, 3)), ((0, 3), (1, 2)))
-VARIANTS = ((0, 6, 6), (0, 8, 8))
-T_U, T_V, SRC_K, DST_K, SRC_V, DST_V, REQ, FILL, PLAN = 0, 128, 256, 264, 272, 280, 288, 352, 416
+VARIANTS = (
+    (0, 5, 5),
+    (1, 5, 5),
+    (2, 5, 5),
+    (0, 5, 6),
+    (1, 5, 6),
+    (2, 5, 6),
+    (0, 6, 5),
+    (1, 6, 5),
+    (2, 6, 5),
+    (0, 6, 6),
+    (1, 6, 6),
+    (2, 6, 6),
+    (0, 7, 7),
+    (0, 8, 8),
+)
+SEND, SOURCE, DEST, REQ, FILL = 0, 2, 4, 6, 7
 
 
 def hadamard(order_size):
@@ -59,8 +74,8 @@
             q_low, keys, (((1,), (1,)), ((), ())), preferred_element_type=jnp.float32
         )
         for c in range(CHUNK):
-            req = plan_ref[REQ + i * CHUNK + c]
-            fill = plan_ref[FILL + i * CHUNK + c]
+            req = plan_ref[REQ, i * CHUNK + c]
+            fill = plan_ref[FILL, i * CHUNK + c]
             live = (row_req == req) & (token < fill)
             part = jnp.where(live, s[:, c * BT : (c + 1) * BT] * scale, NEG_FILL)
             scores[i, :, c * BT : (c + 1) * BT] = part
@@ -129,9 +144,145 @@
     return jnp.bitwise_xor(gx, gx // 2) * 8 + jnp.bitwise_xor(gy, gy // 2) * 2 + core
 
 
+def lanes_to_rows(row, count):
+    sub = lax.broadcasted_iota(jnp.int32, (count, 128), 0)
+    lane = lax.broadcasted_iota(jnp.int32, (count, 128), 1)
+    return jnp.sum(jnp.where(sub == lane, row, 0), axis=1, keepdims=True)
+
+
+def moved_elements(dest):
+    sub = lax.broadcasted_iota(jnp.int32, (16, 128), 0)
+    lane = lax.broadcasted_iota(jnp.int32, (16, 128), 1)
+    return (dest != 2 * sub + lane // 64).astype(jnp.int32)
+
+
+def released_row(dest):
+    moved = moved_elements(dest)
+    sub = lax.broadcasted_iota(jnp.int32, (16, 128), 0)
+    lane = lax.broadcasted_iota(jnp.int32, (16, 128), 1)
+    pick = jnp.where(lane % 2 == 0, moved[:, 0:1], moved[:, 64:65])
+    return jnp.sum(jnp.where(lane // 2 == sub, pick, 0), axis=0, keepdims=True)
+
+
+def own_half(ref, me):
+    row = ref[pl.ds(me // 2, 1), :]
+    return jnp.where(me % 2 == 1, jnp.concatenate([row[:, 64:], row[:, :64]], axis=1), row)
+
+
+def write_plan(split, me, dest_ref, req_ref, fill_ref, plan):
+    dest = dest_ref[...]
+    sub = lax.broadcasted_iota(jnp.int32, (32, 128), 0)
+    lane = lax.broadcasted_iota(jnp.int32, (32, 128), 1)
+    sub_all = lax.broadcasted_iota(jnp.int32, (128, 128), 0)
+    lane_all = lax.broadcasted_iota(jnp.int32, (128, 128), 1)
+    gone_row = released_row(dest)
+    kept_row = jnp.where(lane[:1] < INST, 1 - gone_row, 0)
+    gone = lanes_to_rows(gone_row, 32)
+    at_row = coordinates(lane, split)
+    at_col = coordinates(sub, split)
+    at_me = coordinates(me, split)
+    own = own_half(dest_ref, me)
+    own_col = lanes_to_rows(own, 128)
+    rank = jnp.sum(
+        ((own_col == own) & (sub_all < lane_all)).astype(jnp.int32), axis=0, keepdims=True
+    )
+    for plane in range(2):
+        one, two = plane, 1 - plane
+        kept_rank = jnp.sum(
+            jnp.where((at_col[one] == at_row[one]) & (lane < sub), kept_row, 0),
+            axis=1,
+            keepdims=True,
+        )
+        gone_rank = jnp.sum(
+            jnp.where((at_col[two] == at_row[two]) & (lane < sub), gone_row, 0),
+            axis=1,
+            keepdims=True,
+        )
+        place = at_col[one] * 32 + kept_rank * PER
+        at = jnp.sum(jnp.where(sub == own, place, 0), axis=0, keepdims=True) + rank
+        at = jnp.where(lane[:1] < SLOTS, at, -1)
+        hit = lanes_to_rows(at, 128) == lane_all
+        plan[SEND + plane : SEND + plane + 1] = jnp.sum(
+            jnp.where(hit, sub_all, 0), axis=0, keepdims=True
+        )
+        source = (jnp.bitwise_xor(at_col[one], at_me[one]) * 2 + at_col[2]) * GROUP
+        take = (gone == 1) & (at_col[two] == at_me[two]) & (gone_rank == lane)
+        plan[SOURCE + plane : SOURCE + plane + 1] = jnp.sum(
+            jnp.where(take, source, 0), axis=0, keepdims=True
+        )
+        distance = jnp.bitwise_xor(at_col[two], at_me[two]) * 2 + at_col[2]
+        take = (at_col[one] == at_me[one]) & (distance == lane)
+        plan[DEST + plane : DEST + plane + 1] = jnp.sum(
+            jnp.where(take, kept_rank, 0), axis=0, keepdims=True
+        )
+    plan[REQ : REQ + 1] = own_half(req_ref, me)
+    plan[FILL : FILL + 1] = own_half(fill_ref, me)
+
+
+def arrival_table(split, me, dest, slot):
+    sub = lax.broadcasted_iota(jnp.int32, (16, 128), 0)
+    lane = lax.broadcasted_iota(jnp.int32, (16, 128), 1)
+    source = 2 * sub + lane // 64
+    to_me = (dest == me) & (moved_elements(dest) == 1)
+    count = to_me.astype(jnp.int32)
+    for step in (1, 2, 4, 8, 16, 32):
+        shifted = jnp.concatenate([count[:, 128 - step :], count[:, : 128 - step]], axis=1)
+        count = count + jnp.where(lane % 64 >= step, shifted, 0)
+    rank = count - 1
+    gone_row = released_row(dest)
+    at_row = coordinates(lane, split)
+    at_me = coordinates(me, split)
+    landed = jnp.zeros((16, 128), jnp.int32)
+    for plane in range(2):
+        two = 1 - plane
+        ranks = []
+        for core in range(2):
+            inst = 2 * sub + core
+            same = (coordinates(inst, split)[two] == at_row[two]) & (lane < inst)
+            ranks.append(jnp.sum(jnp.where(same, gone_row, 0), axis=1, keepdims=True))
+        gone_rank = jnp.where(lane < 64, ranks[0], ranks[1])
+        far = jnp.bitwise_xor(coordinates(source, split)[two], at_me[two])
+        row = far * 2 * GROUP + gone_rank + rank // 2 * GROUP + rank % 2 * 8 * GROUP
+        landed = landed * 128 + row
+    landed = jnp.where(to_me, landed, -1)
+    want = lax.broadcasted_iota(jnp.int32, (SLOTS, 128), 0)
+    found = jnp.full((SLOTS, 128), -1, jnp.int32)
+    for i in range(16):
+        found = jnp.maximum(
+            found, jnp.where(slot[i : i + 1] == want, landed[i : i + 1], -1)
+        )
+    column = jnp.max(found, axis=1, keepdims=True)
+    spread = jnp.where(want == lax.broadcasted_iota(jnp.int32, (SLOTS, 128), 1), column + 1, 0)
+    return jnp.broadcast_to(jnp.sum(spread, axis=0, keepdims=True) - 1, (8, 128))
+
+
+def choose_kernel(dest_ref, choice_ref):
+    gone = [(dest_ref[inst * SLOTS] != inst).astype(jnp.int32) for inst in range(INST)]
+    groups = static_groups()
+    need = []
+    for split in range(len(SPLITS)):
+        counts = []
+        for coord in range(2):
+            for group in range(4):
+                members = [gone[i] for i in range(INST) if groups[split][coord][i] == group]
+                counts.append(functools.reduce(jnp.add, members))
+        most = functools.reduce(jnp.maximum, counts)
+        least = functools.reduce(jnp.minimum, counts)
+        need.append((8 - least, most))
+    choice = jnp.full((), len(VARIANTS) - 1, jnp.int32)
+    for index in reversed(range(len(VARIANTS) - 1)):
+        split, cap1, cap2 = VARIANTS[index]
+        fits = (need[split][0] <= cap1) & (need[split][1] <= cap2)
+        choice = jnp.where(fits, index, choice)
+    choice_ref[0] = choice
+
+
 def layer_kernel(split, cap1, cap2, *refs):
     (
-        plan_ref,
+        dest_ref,
+        slot_ref,
+        req_ref,
+        fill_ref,
         q_ref,
         nk_ref,
         nv_ref,
@@ -140,8 +291,11 @@
         ck_ref,
         cv_ref,
         out_ref,
+        table_ref,
         rk_ref,
         rv_ref,
+        plan_vmem,
+        plan_ref,
         kc,
         vc,
         first_send,
@@ -157,6 +311,7 @@
         att,
         proj,
         load_sem,
+        plan_sem,
         first_s,
         first_r,
         second_s,
@@ -176,9 +331,6 @@
     caches = (kc, vc)
     mids = ((mid_k0, mid_k1), (mid_v0, mid_v1))
     lands = (rk_ref, rv_ref)
-    tables = (T_U, T_V)
-    sources = (SRC_K, SRC_V)
-    dests = (DST_K, DST_V)
 
     load_k = pltpu.make_async_copy(ck_ref, kc, load_sem.at[0])
     load_v = pltpu.make_async_copy(cv_ref, vc, load_sem.at[1])
@@ -201,6 +353,10 @@
 
     lax.fori_loop(1, INST, greet_inst, 0)
     lax.fori_loop(1, HEADS, greet_head, 0)
+
+    write_plan(split, me, dest_ref, req_ref, fill_ref, plan_vmem)
+    to_smem = pltpu.make_async_copy(plan_vmem, plan_ref, plan_sem)
+    to_smem.start()
 
     sign_row = (2 * signs_ref[...] - 1).astype(jnp.float32)
     rotate = hadamard(HD)
@@ -213,6 +369,7 @@
     ) * (1.0 / math.sqrt(HD))
     q_low = q_rot.astype(jnp.bfloat16)
 
+    to_smem.wait()
     load_k.wait()
     load_v.wait()
     pl.semaphore_wait(barrier, INST - 1 + HEADS - 1)
@@ -262,7 +419,7 @@
             for plane in range(2):
                 first = jnp.bitwise_xor(u if plane == 0 else v, d)
                 for m in range(cap1):
-                    b = plan_ref[tables[plane] + first * 32 + m * PER + j * 2 + half]
+                    b = plan_ref[SEND + plane, first * 32 + m * PER + j * 2 + half]
                     first_send[plane, half, d * 2 + j, m] = caches[plane][b]
 
                 @pl.when((d > 0) | (j != core))
@@ -288,9 +445,9 @@
         def body(t, _):
             d, j = 3 - t // 2, t % 2
             for plane in range(2):
-                base = plan_ref[dests[plane] + d * 2 + j]
+                base = plan_ref[DEST + plane, d * 2 + j]
                 for n in range(cap2):
-                    b = base + plan_ref[sources[plane] + n]
+                    b = base + plan_ref[SOURCE + plane, n]
                     second_send[plane, half, d * 2 + j, n] = mids[plane][half][b]
 
                 @pl.when((d > 0) | (j != core))
@@ -329,6 +486,7 @@
     def _():
         part_copy(0).start()
 
+    table_ref[...] = arrival_table(split, me, dest_ref[...], slot_ref[...])
     start_second(0)
 
     @pl.when(core == 0)
@@ -476,10 +634,17 @@
 
     return pl.pallas_call(
         functools.partial(layer_kernel, split, cap1, cap2),
-        out_shape=(jax.ShapeDtypeStruct((16, 256), jnp.float32), blocks, blocks),
-        in_specs=[smem, vmem, vmem, vmem, vmem, vmem, hbm, hbm],
-        out_specs=(vmem, hbm, hbm),
+        out_shape=(
+            jax.ShapeDtypeStruct((16, 256), jnp.float32),
+            jax.ShapeDtypeStruct((8, 128), jnp.int32),
+            blocks,
+            blocks,
+        ),
+        in_specs=[vmem] * 9 + [hbm, hbm],
+        out_specs=(vmem, vmem, hbm, hbm),
         scratch_shapes=[
+            pltpu.VMEM((8, 128), jnp.int32),
+            pltpu.SMEM((8, 128), jnp.int32),
             low(SLOTS),
             low(SLOTS),
             low(2, 2, 8, cap1),
@@ -495,6 +660,7 @@
             pltpu.VMEM((16, 8, HD), jnp.float32),
             pltpu.VMEM((HEADS, 16, 256), jnp.float32),
             dma((2,)),
+            dma,
             dma((2, 2, 8)),
             dma((2, 2, 8)),
             dma((2, 2, 8)),
@@ -517,7 +683,8 @@
 
     def place(s, _):
         for plane, (src, dst) in enumerate(lands):
-            row = table_ref[plane * SLOTS + s]
+            landed = table_ref[0, s]
+            row = jnp.where(landed < 0, -1, landed // 128 if plane == 0 else landed % 128)
 
             @pl.when(row >= 0)
             def _(plane=plane, src=src, dst=dst, row=row):
@@ -534,7 +701,8 @@
 
     def settle(s, _):
         for plane, (src, dst) in enumerate(lands):
-            row = table_ref[plane * SLOTS + s]
+            landed = table_ref[0, s]
+            row = jnp.where(landed < 0, -1, landed // 128 if plane == 0 else landed % 128)
 
             @pl.when(row >= 0)
             def _(plane=plane, src=src, dst=dst, row=row):
@@ -556,89 +724,6 @@
             rows.append((bits[a0] + 2 * bits[a1], bits[b0] + 2 * bits[b1]))
         out.append(np.array(rows, np.int32).T)
     return np.stack(out)
-
-
-def move_plan(own, block_req, block_fill, dest_inst, new_slot):
-    i32 = jnp.int32
-    peers = jnp.arange(INST, dtype=i32)
-    slots = jnp.arange(SLOTS, dtype=i32)
-    dest = dest_inst.reshape(INST, SLOTS)
-    slot_of = new_slot.reshape(INST, SLOTS)
-    released = dest[:, 0] != peers
-    groups = static_groups()
-
-    def needs(split):
-        u, v = jnp.asarray(groups[split])
-        most_kept, most_gone = jnp.zeros((), i32), jnp.zeros((), i32)
-        for coord in (u, v):
-            inside = coord[None, :] == jnp.arange(4, dtype=i32)[:, None]
-            gone = jnp.sum((inside & released[None, :]).astype(i32), axis=1)
-            most_gone = jnp.maximum(most_gone, jnp.max(gone))
-            most_kept = jnp.maximum(most_kept, 8 - jnp.min(gone))
-        return most_kept, most_gone
-
-    need = {split: needs(split) for split in sorted({variant[0] for variant in VARIANTS})}
-    choice = jnp.full((), len(VARIANTS) - 1, i32)
-    for index in reversed(range(len(VARIANTS) - 1)):
-        split, cap1, cap2 = VARIANTS[index]
-        fits = (need[split][0] <= cap1) & (need[split][1] <= cap2)
-        choice = jnp.where(fits, index, choice)
-    used = [split for split, _, _ in VARIANTS]
-    coords = jnp.asarray(groups[used[-1]])
-    for index in range(len(VARIANTS) - 1):
-        if used[index] != used[-1]:
-            coords = jnp.where(choice == index, jnp.asarray(groups[used[index]]), coords)
-    core = peers % 2
-    mine = (peers == own).astype(i32)
-    before = peers[None, :] < peers[:, None]
-    own_dest = jnp.sum(dest * mine[:, None], axis=0)
-    own_rank = jnp.sum(
-        ((own_dest[:, None] == own_dest[None, :]) & (slots[None, :] < slots[:, None])).astype(i32),
-        axis=1,
-    )
-    to_me = (dest == own) & released[:, None]
-    rank = jnp.sum(
-        (to_me[:, None, :] & (slots[None, None, :] < slots[None, :, None])).astype(i32), axis=2
-    )
-    sends, extras, rows = [], [], []
-    for plane in range(2):
-        first, second = (coords[0], coords[1]) if plane == 0 else (coords[1], coords[0])
-        own_first, own_second = jnp.sum(first * mine), jnp.sum(second * mine)
-        kept_rank = jnp.sum(
-            ((first[:, None] == first[None, :]) & before & ~released[None, :]).astype(i32), axis=1
-        )
-        gone_rank = jnp.sum(
-            ((second[:, None] == second[None, :]) & before & released[None, :]).astype(i32), axis=1
-        )
-        place = first * 32 + kept_rank * PER
-        sent = jnp.sum(
-            jnp.where(own_dest[:, None] == peers[None, :], place[None, :], 0), axis=1
-        )
-        at = sent + own_rank
-        hit = at[None, :] == jnp.arange(128, dtype=i32)[:, None]
-        sends.append(jnp.sum(jnp.where(hit, slots[None, :], 0), axis=1))
-        lane = jnp.arange(8, dtype=i32)[:, None]
-        source = (jnp.bitwise_xor(first, own_first) * 2 + core) * GROUP
-        take = released & (second == own_second)
-        extras.append(
-            jnp.sum(jnp.where(take[None, :] & (gone_rank[None, :] == lane), source[None, :], 0), 1)
-        )
-        distance = jnp.bitwise_xor(second, own_second) * 2 + core
-        take = first == own_first
-        extras.append(
-            jnp.sum(jnp.where(take[None, :] & (distance[None, :] == lane), kept_rank[None, :], 0), 1)
-        )
-        base = jnp.bitwise_xor(second, own_second) * 2 * GROUP + gone_rank
-        rows.append(
-            base[:, None] + (rank // 2) * GROUP + (rank % 2) * 8 * GROUP
-        )
-    lands = to_me[None] & (slot_of[None] == slots[:, None, None])
-    table = [
-        jnp.max(jnp.where(lands, row[None], -1), axis=(1, 2)) for row in rows
-    ]
-    own_req = jnp.sum(block_req.reshape(INST, SLOTS) * mine[:, None], axis=0)
-    own_fill = jnp.sum(block_fill.reshape(INST, SLOTS) * mine[:, None], axis=0)
-    return choice, jnp.concatenate([*sends, *extras, own_req, own_fill]), jnp.concatenate(table)
 
 
 def shards(
@@ -654,10 +739,20 @@
     new_slot,
     out_weight,
 ):
-    own = lax.axis_index("inst")
-    choice, plan, table = move_plan(own, block_req, block_fill, dest_inst, new_slot)
+    vmem = pl.BlockSpec(memory_space=pltpu.VMEM)
+    smem = pl.BlockSpec(memory_space=pltpu.SMEM)
+    hbm = pl.BlockSpec(memory_space=pl.ANY)
+    choice = pl.pallas_call(
+        choose_kernel,
+        out_shape=jax.ShapeDtypeStruct((1,), jnp.int32),
+        in_specs=[smem],
+        out_specs=smem,
+    )(dest_inst)[0]
     operands = (
-        plan,
+        dest_inst.reshape(16, 128),
+        new_slot.reshape(16, 128),
+        block_req.reshape(16, 128),
+        block_fill.reshape(16, 128),
         query.reshape(ROWS, HD),
         new_keys.reshape(16, HD),
         new_values.reshape(16, HD),
@@ -667,10 +762,7 @@
         cache_values.reshape(SLOTS, BT, HD),
     )
     branches = [functools.partial(layer_call, variant) for variant in range(len(VARIANTS))]
-    proj, got_keys, got_values = lax.switch(choice, branches, operands)
-    vmem = pl.BlockSpec(memory_space=pltpu.VMEM)
-    smem = pl.BlockSpec(memory_space=pltpu.SMEM)
-    hbm = pl.BlockSpec(memory_space=pl.ANY)
+    proj, table, got_keys, got_values = lax.switch(choice, branches, operands)
     layer_out, moved_keys, moved_values = pl.pallas_call(
         place_kernel,
         out_shape=(

time: 137 us -> 100 us (0.73)
  Pallas kernels: 113 us -> 93.2 us
  other arithmetic: 16.6 us -> 0 us
  loops' own time: 0.01 us -> 5.3 us
  local copies, waits for them, and re-layouts: 3.27 us -> 0 us
  between operations: 3.24 us -> 1.51 us
    pallas_call x1, Pallas kernels: 108 us -> 85.4 us  [layer_call(): pl.pallas_call(functools.partial(layer_kernel, split, cap1, cap2), out_sh...]
    reduce_sum x12 -> x0, other arithmetic: 5.84 us -> none  [the longest x2 2.59 us: move_plan(): own_first, own_second = (jnp.sum(first * mine), jnp.sum(second * mine))]
    another operation x1, loops' own time: 0.01 us -> 5.3 us  [shards(): proj, table, got_keys, got_values = lax.switch(choice, branches, operands)]
    reduce_max x2 -> x0, other arithmetic: 3.14 us -> none  [the longest x1 2.41 us: move_plan(): jnp.max(jnp.where(lands, row[None], -1), axis=(1, 2))]
    add x4 -> x0, other arithmetic: 2.74 us -> none  [the longest x1 1.97 us: move_plan(): base = jnp.bitwise_xor(second, own_second) * 2 * GROUP + gone_rank]
    reshape x3 -> x0, local copies, waits for them, and re-layouts: 2.3 us -> none  [the longest x1 0.77 us: move_plan(): dest = dest_inst.reshape(INST, SLOTS)]
    and x2 -> x0, other arithmetic: 2.05 us -> none  [the longest x1 1.97 us: move_plan(): take[None, :] & (distance[None, :] == lane)]
    pallas_call x0 -> x1, Pallas kernels: none -> 1.46 us  [shards(): pl.pallas_call(choose_kernel, out_shape=jax.ShapeDtypeStruct((1,), jnp.in...]
where the time goes in v3:
time: 100 us
  Pallas kernels  93.2 us (93%)
  loops' own time  5.3 us (5%)
  between operations  1.51 us (2%)
    pallas_call x1, Pallas kernels, layer_call(): pl.pallas_call(functools.partial(layer_kernel, split, cap1, cap2), out_sh...  85.4 us
    pallas_call x1, Pallas kernels, shards(): pl.pallas_call(place_kernel, out_shape=(jax.ShapeDtypeStruct((16, 256), j...  6.4 us
    another operation x1, loops' own time, shards(): proj, table, got_keys, got_values = lax.switch(choice, branches, operands)  5.3 us

profile of v3, /device:TPU:1, one launch (start us, length us, event | category | flops | bytes accessed | tf_op | source)
XLA Modules:
  0.0 100.0 jit_solution(11988887733556149971)
XLA Ops:
  0.6 1.5 %shard_map.130 = s32[1]{0:T(128)} custom-call(s32[2048]{0:T(1024)} %dest_ref.1), custom_call_target="tpu_custom_call" | custom-call | tf_op jit(solution)/shard_map/pallas_call | solution.py:745
  2.7 90.7 %conditional.1 = ((f32[16,256]{1,0:T(8,128)S(1)}, s32[8,128]{1,0:T(8,128)S(1)}, bf16[128,128,128]{2,1,0:T(8,128)(2,1)}, bf16[128,128,128]{2,1,0:T(8,128)(2,1)})) conditional(s32[]{:T(128)} %bitcast, (s32[16,128]{1,0:T(8,128)}, s32[16,128]{1,0:T(8,128)}, s32[16,128]{1,0:T(8,128)}, s32[16,128]{1,0:T(8,128)}, ...), branch_computations={%region_0.0_spmd, %region_1.0_spmd, %region_2.0_spmd, %region_3.0_... | conditional | bytes 8 | solution.py:765
  3.0 85.4 %branch_10_fun.1 = (f32[16,256]{1,0:T(8,128)S(1)}, s32[8,128]{1,0:T(8,128)S(1)}, bf16[128,128,128]{2,1,0:T(8,128)(2,1)}, bf16[128,128,128]{2,1,0:T(8,128)(2,1)}) custom-call(s32[16,128]{1,0:T(8,128)} %get-tuple-element.418.refs_0_, s32[16,128]{1,0:T(8,128)} %get-tuple-element.419.refs_1_, s32[16,128]{1,0:T(8,128)} %get-tuple-element.420.refs_2_, ...), custom_call_target="tpu_custom_call" | custom-call | tf_op jit(solution)/shard_map/cond/branch_10_fun/pallas_call | solution.py:635
  93.4 6.4 %shard_map.131 = (bf16[16,256]{1,0:T(8,128)(2,1)}, bf16[64,128,128]{2,1,0:T(8,128)(2,1)}, bf16[64,128,128]{2,1,0:T(8,128)(2,1)}) custom-call(s32[8,128]{1,0:T(8,128)S(1)} %get-tuple-element.472.table_ref, f32[16,256]{1,0:T(8,128)S(1)} %get-tuple-element.473.proj_ref, bf16[128,128,128]{2,1,0:T(8,128)(2,1)} %get-tuple-element.474.rk_ref, ...), custom_call_target="tpu_custom_call" | custom-call | tf_op jit(solution)/shard_map/pallas_call | solution.py:766

commit v4 on v3

--- a/solution.py
+++ b/solution.py
@@ -351,8 +351,8 @@
         )
         return 0
 
+    lax.fori_loop(1, HEADS, greet_head, 0)
     lax.fori_loop(1, INST, greet_inst, 0)
-    lax.fori_loop(1, HEADS, greet_head, 0)
 
     write_plan(split, me, dest_ref, req_ref, fill_ref, plan_vmem)
     to_smem = pltpu.make_async_copy(plan_vmem, plan_ref, plan_sem)
@@ -678,39 +678,56 @@
     )(*operands)
 
 
-def place_kernel(table_ref, proj_ref, rk_ref, rv_ref, out_ref, mk_ref, mv_ref, sems):
+def place_kernel(
+    table_ref, proj_ref, rk_ref, rv_ref, out_ref, mk_ref, mv_ref, placed, in_sems, out_sems
+):
     lands = ((rk_ref, mk_ref), (rv_ref, mv_ref))
-
-    def place(s, _):
-        for plane, (src, dst) in enumerate(lands):
-            landed = table_ref[0, s]
-            row = jnp.where(landed < 0, -1, landed // 128 if plane == 0 else landed % 128)
-
-            @pl.when(row >= 0)
-            def _(plane=plane, src=src, dst=dst, row=row):
-                pltpu.make_async_copy(src.at[row], dst.at[s], sems.at[plane]).start()
-
-            @pl.when(row < 0)
-            def _(dst=dst):
-                dst[s] = jnp.zeros((BT, HD), jnp.bfloat16)
-
-        return 0
-
-    lax.fori_loop(0, SLOTS, place, 0)
+    parts, width = 4, SLOTS // 4
+
+    def store(plane, src_plane, part):
+        rows = pl.ds(part * width, width)
+        return pltpu.make_async_copy(
+            placed.at[src_plane, rows], lands[plane][1].at[rows], out_sems.at[plane, part]
+        )
+
+    kept = table_ref[0, 0] >= 0
+
+    @pl.when(kept)
+    def _():
+        for part in range(parts):
+
+            def fetch(t, _):
+                s = part * width + t
+                landed = table_ref[0, s]
+                for plane, row in enumerate((landed // 128, landed % 128)):
+                    pltpu.make_async_copy(
+                        lands[plane][0].at[row], placed.at[plane, s], in_sems.at[plane, part]
+                    ).start()
+                return 0
+
+            lax.fori_loop(0, width, fetch, 0, unroll=4)
+        for part in range(parts):
+            rows = pl.ds(part * width, width)
+            for plane in range(2):
+                pltpu.make_async_copy(
+                    lands[plane][0].at[rows], placed.at[plane, rows], in_sems.at[plane, part]
+                ).wait()
+                store(plane, plane, part).start()
+
+    @pl.when(jnp.logical_not(kept))
+    def _():
+        placed[0, :width] = jnp.zeros((width, BT, HD), jnp.bfloat16)
+        for plane in range(2):
+            for part in range(parts):
+                rows = pl.ds(part * width, width)
+                pltpu.make_async_copy(
+                    placed.at[0, pl.ds(0, width)], lands[plane][1].at[rows], out_sems.at[plane, part]
+                ).start()
+
     out_ref[...] = proj_ref[...].astype(jnp.bfloat16)
-
-    def settle(s, _):
-        for plane, (src, dst) in enumerate(lands):
-            landed = table_ref[0, s]
-            row = jnp.where(landed < 0, -1, landed // 128 if plane == 0 else landed % 128)
-
-            @pl.when(row >= 0)
-            def _(plane=plane, src=src, dst=dst, row=row):
-                pltpu.make_async_copy(src.at[row], dst.at[s], sems.at[plane]).wait()
-
-        return 0
-
-    lax.fori_loop(0, SLOTS, settle, 0)
+    for plane in range(2):
+        for part in range(parts):
+            store(plane, plane, part).wait()
 
 
 def static_groups():
@@ -771,10 +788,19 @@
             jax.ShapeDtypeStruct((SLOTS, BT, HD), jnp.bfloat16),
         ),
         in_specs=[smem, vmem, hbm, hbm],
-        out_specs=(vmem, vmem, vmem),
-        scratch_shapes=[pltpu.SemaphoreType.DMA((2,))],
+        out_specs=(vmem, hbm, hbm),
+        scratch_shapes=[
+            pltpu.VMEM((2, SLOTS, BT, HD), jnp.bfloat16),
+            pltpu.SemaphoreType.DMA((2, 4)),
+            pltpu.SemaphoreType.DMA((2, 4)),
+        ],
         compiler_params=pltpu.CompilerParams(vmem_limit_bytes=32 * 2**20),
-    )(table, proj, got_keys, got_values)
+    )(
+        table,
+        proj,
+        got_keys,
+        got_values,
+    )
     return (
         layer_out.reshape(2, 8, 256),
         moved_keys.reshape(SLOTS, BT, 1, HD),

time: 100 us -> 93.9 us (0.939)
  loops' own time: 5.3 us -> 0.58 us
  Pallas kernels: 93.2 us -> 91.2 us
    another operation x1, loops' own time: 5.3 us -> 0.58 us  [shards(): proj, table, got_keys, got_values = lax.switch(choice, branches, operands)]
    pallas_call x1, Pallas kernels: 6.4 us -> 4.79 us  [shards(): pl.pallas_call(place_kernel, out_shape=(jax.ShapeDtypeStruct((16, 256), j...]
where the time goes in v4:
time: 93.9 us; the launch traced here: 93.3 us
  Pallas kernels  91.2 us (97%)
  between operations  1.51 us (2%)
    pallas_call x1, Pallas kernels, layer_call(): pl.pallas_call(functools.partial(layer_kernel, split, cap1, cap2), out_sh...  84.9 us
    pallas_call x1, Pallas kernels, shards(): pl.pallas_call(place_kernel, out_shape=(jax.ShapeDtypeStruct((16, 256), j...  4.79 us

profile of v4, /device:TPU:1, one launch (start us, length us, event | category | flops | bytes accessed | tf_op | source)
XLA Modules:
  0.0 93.3 jit_solution(17148880398556880072)
XLA Ops:
  0.6 1.5 %shard_map.130 = s32[1]{0:T(128)} custom-call(s32[2048]{0:T(1024)} %dest_ref.1), custom_call_target="tpu_custom_call" | custom-call | tf_op jit(solution)/shard_map/pallas_call | solution.py:762
  2.7 85.5 %conditional.1 = ((f32[16,256]{1,0:T(8,128)S(1)}, s32[8,128]{1,0:T(8,128)S(1)}, bf16[128,128,128]{2,1,0:T(8,128)(2,1)}, bf16[128,128,128]{2,1,0:T(8,128)(2,1)})) conditional(s32[]{:T(128)} %bitcast, (s32[16,128]{1,0:T(8,128)}, s32[16,128]{1,0:T(8,128)}, s32[16,128]{1,0:T(8,128)}, s32[16,128]{1,0:T(8,128)}, ...), branch_computations={%region_0.0_spmd, %region_1.0_spmd, %region_2.0_spmd, %region_3.0_... | conditional | bytes 8 | solution.py:782
  3.0 84.9 %branch_9_fun.1 = (f32[16,256]{1,0:T(8,128)S(1)}, s32[8,128]{1,0:T(8,128)S(1)}, bf16[128,128,128]{2,1,0:T(8,128)(2,1)}, bf16[128,128,128]{2,1,0:T(8,128)(2,1)}) custom-call(s32[16,128]{1,0:T(8,128)} %get-tuple-element.407.refs_0_, s32[16,128]{1,0:T(8,128)} %get-tuple-element.408.refs_1_, s32[16,128]{1,0:T(8,128)} %get-tuple-element.409.refs_2_, ...), custom_call_target="tpu_custom_call" | custom-call | tf_op jit(solution)/shard_map/cond/branch_9_fun/pallas_call | solution.py:635
  88.2 4.8 %shard_map.131 = (bf16[16,256]{1,0:T(8,128)(2,1)}, bf16[64,128,128]{2,1,0:T(8,128)(2,1)}, bf16[64,128,128]{2,1,0:T(8,128)(2,1)}) custom-call(s32[8,128]{1,0:T(8,128)S(1)} %get-tuple-element.472.table_ref, f32[16,256]{1,0:T(8,128)S(1)} %get-tuple-element.473.proj_ref, bf16[128,128,128]{2,1,0:T(8,128)(2,1)} %get-tuple-element.474.rk_ref, ...), custom_call_target="tpu_custom_call" | custom-call | tf_op jit(solution)/shard_map/pallas_call | solution.py:783
